TPU v7x, 256 devices: a whole 4x4x8 slice. The times are simulated.
256 devices in a mesh: rep: 16 (over y_hi, z), loop: 8 (over x, core), seq: 2 (over y_lo).
Axes of the slice: x: 4, y: 4 (y_hi: 2, y_lo: 2; y = y_hi * 2 + y_lo), z: 8, core: 2. Of those that a mesh axis runs over, the one named last changes fastest.
Arguments:
- patches: bfloat16 [512, 256, 1152], P(('rep', 'loop', 'seq')), may hold values from -6 to 6
- positions: int32 [2, 512, 256], P(None, ('rep', 'loop', 'seq')), may hold values from 0 to 127, as said below
- counts: int32 [512], P(('rep', 'loop', 'seq')), may hold values from 2 to 256, as said below
- probe: bfloat16 [1152], replicated
- w_keyval: bfloat16 [1152, 2304], replicated, may hold values from -0.1875 to 0.1875
- w_out: bfloat16 [1152, 1152], replicated, may hold values from -0.1875 to 0.1875
- texts: bfloat16 [512, 1152], P(('rep', 'loop'), 'seq'), may hold values from -0.1875 to 0.1875
Outputs:
- txt_grad: float32 [512, 1152], P(('rep', 'loop'), 'seq')
- wo_grad: float32 [1152, 1152], P(('rep', 'loop'), 'seq')
Inputs may be any that keep to these rules, and one draw needn't show every extreme that they name: `counts`: each image's patches fill a grid of c columns (2 to 32) and r rows, row by row; its count is r * c. Images whose index is a multiple of 4 fill all 256 slots, and so do those whose index is 1 more than a multiple of 4. `positions`: for slot p below the image's count, the row is p // c and the column p % c of that image's c columns; beyond it both are 0.
All inputs are finite; a program needn't handle non-finite values.
Results may differ from a plain program's by a relative error of at most 0.012.
Values may be sent and summed in bfloat16 or wider, within the bound.
No kernel may reach another device: no remote copies, remote signals or barrier semaphores. Data moves between devices by JAX's collectives and lax.ppermute only.
A program may use at most 64 MiB of HBM per device.

v0:
```python
import math

import jax
import jax.numpy as jnp
from jax import lax
from jax.sharding import PartitionSpec as P

HEADS = 16
HEAD_DIM = 72


MASK_FILL = -1e30
LOGIT_SCALE = 10.0
LOGIT_BIAS = -2.0


def shifted(value, axis, steps):
    count = lax.axis_size(axis)
    pairs = [(source, (source + steps) % count) for source in range(count)]
    return lax.ppermute(value, axis, pairs)


def rotate_keys(key_rows, row_pos, col_pos):
    count = key_rows.shape[0]
    quarter = HEAD_DIM // 4
    blocks = key_rows.reshape(count, HEADS, 2, 2, quarter)
    freqs = jnp.exp(jnp.arange(quarter, dtype=jnp.float32) * (-math.log(10000.0) / quarter))
    angles = jnp.stack([row_pos, col_pos], axis=1).astype(jnp.float32)[:, :, None] * freqs
    cosine = jnp.cos(angles)[:, None]
    sine = jnp.sin(angles)[:, None]
    first_half = blocks[:, :, :, 0]
    second_half = blocks[:, :, :, 1]
    turned = jnp.stack(
        [first_half * cosine - second_half * sine, first_half * sine + second_half * cosine], axis=3
    )
    return turned.reshape(count, HEADS * HEAD_DIM)


def inner_rows(left, right):
    return lax.dot_general(
        left, right, (((1,), (1,)), ((), ())), preferred_element_type=jnp.float32
    )


def outer_rows(left, right):
    return lax.dot_general(
        left, right, (((0,), (0,)), ((), ())), preferred_element_type=jnp.float32
    )


def pair_grads(labels, inner_sum):
    logit = LOGIT_SCALE * inner_sum + LOGIT_BIAS
    return (LOGIT_SCALE * (-labels * jax.nn.sigmoid(-labels * logit))).astype(jnp.bfloat16)


def local(patches, positions, counts, probe, w_keyval, w_out, texts):
    images, slots, width = patches.shape
    key_value = jnp.dot(
        patches.reshape(images * slots, width), w_keyval, preferred_element_type=jnp.float32
    )
    key_rows = rotate_keys(key_value[:, :width], positions[0].reshape(-1), positions[1].reshape(-1))
    value_rows = key_value[:, width:].astype(jnp.bfloat16).reshape(images, slots, HEADS, HEAD_DIM)
    scores = (key_rows * probe.astype(jnp.float32)).reshape(images, slots, HEADS, HEAD_DIM).sum(
        axis=3
    ) * HEAD_DIM ** (-0.5)
    live = (jnp.arange(slots, dtype=jnp.int32)[None, :] < counts[:, None])[:, :, None]
    scores = jnp.where(live, scores, MASK_FILL)
    top = scores.max(axis=1)
    raised = jnp.where(live, jnp.exp(scores - top[:, None]), 0.0)
    total = raised.sum(axis=1)
    weights = raised.astype(jnp.bfloat16)
    summed = jnp.einsum("bph,bphd->bhd", weights, value_rows, preferred_element_type=jnp.float32)
    pooled = (summed / total[:, :, None]).reshape(images, width).astype(jnp.bfloat16)
    projected = jnp.dot(pooled, w_out, preferred_element_type=jnp.float32)
    length = jnp.sqrt(jnp.sum(projected * projected, axis=1, keepdims=True) + 1e-06)
    unit = projected / length
    embedded = unit.astype(jnp.bfloat16)
    text_rows, half_width = texts.shape
    seq_index = lax.axis_index("seq")
    emb_pair_rows = lax.all_gather(embedded, "seq", axis=0, tiled=True)
    emb_half = lax.dynamic_slice_in_dim(emb_pair_rows, seq_index * half_width, half_width, 1)
    diagonal = (
        jnp.arange(text_rows, dtype=jnp.int32)[:, None]
        == jnp.arange(text_rows, dtype=jnp.int32)[None, :]
    )

    def turn(turn_index, carry):
        text_block, text_acc, image_acc = carry
        inner_sum = lax.psum(inner_rows(emb_half, text_block), "seq")
        labels = jnp.where((turn_index == 0) & diagonal, 1.0, -1.0)
        grads_block = pair_grads(labels, inner_sum)
        image_part = jnp.dot(grads_block, text_block, preferred_element_type=jnp.float32)
        text_block, text_acc = (
            shifted(text_block.astype(jnp.float32), "loop", 1).astype(text_block.dtype),
            shifted(text_acc + outer_rows(grads_block, emb_half), "loop", 1),
        )
        return (text_block, text_acc, image_acc + image_part)

    start = (
        texts,
        jnp.zeros((text_rows, half_width), jnp.float32),
        jnp.zeros((text_rows, half_width), jnp.float32),
    )
    final_texts, txt_grad, image_halves = lax.fori_loop(0, lax.axis_size("loop"), turn, start)
    image_grad = lax.all_to_all(image_halves, "seq", split_axis=0, concat_axis=1, tiled=True)
    inner = jnp.sum(unit * image_grad, axis=1, keepdims=True)
    out_grad = ((image_grad - unit * inner) / length).astype(jnp.bfloat16)
    row_block = lax.psum_scatter(
        outer_rows(pooled, out_grad), ("rep", "loop"), scatter_dimension=0, tiled=True
    )
    wo_grad = lax.psum_scatter(
        row_block.astype(jnp.bfloat16), "seq", scatter_dimension=1, tiled=True
    ).astype(jnp.float32)
    return (txt_grad, wo_grad)


def solution(mesh):
    return jax.shard_map(
        local,
        mesh=mesh,
        in_specs=(
            P(("rep", "loop", "seq"), None, None),
            P(None, ("rep", "loop", "seq"), None),
            P(("rep", "loop", "seq")),
            P(),
            P(),
            P(),
            P(("rep", "loop"), "seq"),
        ),
        out_specs=(P(("rep", "loop"), "seq"), P(("rep", "loop"), "seq")),
        check_vma=False,
    )
```

profile of v0, /device:TPU:32, one launch (start us, length us, event | category | flops | bytes accessed | tf_op | source)
XLA Modules:
  0.0 857.0 jit_solution(9785975394454300780)
XLA Ops:
  7.2 6.2 fusion.21
  13.4 1.1 slice.36
  14.6 1.6 slice.25
  16.1 5.7 reshape.101
  21.9 3.1 copy.17
  25.1 3.4 reshape.94
  29.1 2.4 multiply_subtract_fusion
  32.3 2.1 fusion.5
  35.3 4.3 all-gather
  39.8 76.7 %while.18 = (s32[]{:T(128)}, bf16[4,576]{1,0:T(4,128)(2,1)S(1)}, f32[4,576]{1,0:T(4,128)S(1)}, f32[4,576]{1,0:T(4,128)S(1)}, bf16[4,576]{1,0:T(4,128)(2,1)S(1)}, /*index=5*/s32[]{:T(128)}, s32[]{:T(128)}) while((s32[]{:T(128)}, bf16[4,576]{1,0:T(4,128)(2,1)S(1)}, f32[4,576]{1,0:T(4,128)S(1)}, f32[4,576]{1,0:T(4,128)S(1)}, ...), condition=%wide.region_6.7_spmd.clone, body=%wide.region_4.6_spmd.clone.sunk | while | flops 62643 | bytes 120296 | solution.py:104
  39.9 4.9 psum.13
  45.7 3.7 collective-permute-done.1
  49.5 4.9 psum.13
  54.8 4.2 collective-permute-done.1
  59.1 4.9 psum.13
  64.4 4.2 collective-permute-done.1
  68.7 4.9 psum.13
  74.0 4.2 collective-permute-done.1
  78.3 4.9 psum.13
  83.6 4.2 collective-permute-done.1
  87.9 4.9 psum.13
  93.1 4.2 collective-permute-done.1
  97.4 4.9 psum.13
  102.7 4.2 collective-permute-done.1
  107.0 4.9 psum.13
  112.3 4.2 collective-permute-done.1
  117.1 3.2 all-to-all-start
  121.6 2.5 all-to-all-done
  124.4 3.3 fusion.14
  127.6 681.4 %all-reduce.2 = bf16[1152,1152]{1,0:T(8,128)(2,1)} all-reduce(f32[1152,1152]{1,0:T(8,128)} %fusion.14), channel_id=2, replica_groups=mesh['rep'=16,'loop'=8,'seq'=2] {'rep','loop'}, use_global_device_ids=true, to_apply=%region_8.9.clone | all-reduce | flops 1327104 | bytes 7962624
  810.8 37.1 %reduce-scatter.4.cloned.1.call-done = bf16[576,9]{1,0:T(8,128)(2,1)} async-done(((bf16[1152,9]{1,0:T(8,128)(2,1)}), bf16[576,9]{1,0:T(8,128)(2,1)}) %reduce-scatter.4.cloned.1.call-update) | async-done | bytes 10384
  847.9 1.0 copy.27
  (102 shorter events, 11.2 us)
Async XLA Ops:
  7.2 27.5 %copy-start = (bf16[1152,1152]{1,0:T(8,128)(2,1)S(1)}, bf16[1152,1152]{1,0:T(8,128)(2,1)}, u32[]{:S(2)}) copy-start(bf16[1152,1152]{1,0:T(8,128)(2,1)} %param.14) | copy-start | bytes 7962628
  16.1 5.7 copy-start.4
  25.0 3.4 copy-start.3
  25.0 3.4 copy-start.2
  32.3 7.5 copy-start.1
  34.4 85.9 %copy-start.5 = (u32[256]{0:T(256)S(1)}, u32[256]{0:T(256)}, u32[]{:S(2)}) copy-start(u32[256]{0:T(256)} %constant.70) | copy-start | bytes 3076
  39.8 5.9 collective-permute-start
  45.1 4.3 collective-permute-start.1
  49.4 5.4 collective-permute-start
  54.7 4.3 collective-permute-start.1
  59.0 5.4 collective-permute-start
  64.3 4.3 collective-permute-start.1
  68.6 5.4 collective-permute-start
  73.8 4.3 collective-permute-start.1
  78.2 5.4 collective-permute-start
  83.4 4.3 collective-permute-start.1
  87.7 5.4 collective-permute-start
  93.0 4.3 collective-permute-start.1
  97.3 5.4 collective-permute-start
  102.6 4.3 collective-permute-start.1
  106.9 5.4 collective-permute-start
  112.2 4.3 collective-permute-start.1
  117.1 7.0 all-to-all-start
  120.3 727.6 %reduce-scatter.4.cloned.1.call-start = ((), (), s32[]{:S(2)}) async-start(), calls=%async_computation.2 | async-start | bytes 442368
Sparse Core Ops, SparseCore 0:
  810.9 36.9 reduce-scatter.3
where the time goes:
time: 859 us; the launch traced here: 857 us
  blocking collectives  725 us (84%)
  waiting for transfers between devices  72.6 us (8%)
  local copies, waits for them, and re-layouts  20.1 us (2%)
  matrix products  15.9 us (2%)
  between operations  14.9 us (2%)
    unnamed x1, blocking collectives  681 us
    psum x8, blocking collectives, turn(): inner_sum = lax.psum(inner_rows(emb_half, text_block), 'seq')  39.4 us
    unnamed x2, waiting for transfers between devices  37.2 us
    ppermute x16, waiting for transfers between devices, shifted(): return lax.ppermute(value, axis, pairs)  32.9 us
  transfers between devices with their start and end apart: 18, of which 10 were waited for; matrix products, arithmetic and copies ran while one was open for 0% of the time, Pallas kernels for 0%

commit v1 on v0

v1 whole, which is shorter than its diff:
```python
import functools

import jax
import jax.numpy as jnp
import numpy as np
from jax import lax
from jax.experimental import pallas as pl
from jax.experimental.pallas import tpu as pltpu
from jax.sharding import PartitionSpec as P

WIDTH = 1152
HEADS = 16
HEAD_DIM = 72
HALF = HEAD_DIM // 2
QUARTER = HEAD_DIM // 4
SLOTS = 256
IMAGES = 2
POSITIONS = 128

MASK_FILL = -1e30
LOGIT_SCALE = 10.0
LOGIT_BIAS = -2.0

GROUP = 40
CHUNKS = ((0, 256), (256, 512), (512, 768), (768, 1024), (1024, 1152))
PAD_ROWS = 16

BF16 = jnp.bfloat16
F32 = jnp.float32


def angle_table():
    freqs = 10000.0 ** (-np.arange(QUARTER) / QUARTER)
    angles = np.arange(POSITIONS)[:, None] * freqs[None, :]
    table = np.zeros((2 * POSITIONS, 2 * POSITIONS), np.float32)
    for kind, value in enumerate((np.cos(angles), np.sin(angles))):
        high = value.astype(BF16).astype(np.float64)
        for part, entry in enumerate((high, value - high)):
            start = (2 * part + kind) * GROUP
            table[:POSITIONS, start : start + QUARTER] = entry
            table[POSITIONS:, start + QUARTER : start + HALF] = entry
    return table


def dot(left, right, left_axis=1, right_axis=0):
    return lax.dot_general(
        left, right, (((left_axis,), (right_axis,)), ((), ())), preferred_element_type=F32
    )


def split(value):
    high = value.astype(BF16)
    return high, (value - high.astype(F32)).astype(BF16)


def pool_kernel(
    counts, positions, probe, table, texts, patches_hbm, weights_hbm, out,
    patches, w_key, w_val, patch_sem, key_sem, val_sem,
):
    copies = []
    for image in range(IMAGES):
        copies.append(
            pltpu.make_async_copy(
                patches_hbm.at[image],
                patches.at[pl.ds(image * SLOTS, SLOTS)],
                patch_sem.at[image],
            )
        )
    key_copies = [
        pltpu.make_async_copy(
            weights_hbm.at[:, pl.ds(lo, hi - lo)], w_key.at[:, pl.ds(lo, hi - lo)], key_sem.at[n]
        )
        for n, (lo, hi) in enumerate(CHUNKS)
    ]
    val_copy = pltpu.make_async_copy(weights_hbm.at[:, pl.ds(WIDTH, WIDTH)], w_val, val_sem)
    copies[0].start()
    key_copies[0].start()
    copies[1].start()
    for copy in key_copies[1:]:
        copy.start()
    val_copy.start()

    pos = jnp.concatenate([positions[0], positions[1], jnp.zeros((4, SLOTS), jnp.int32)], axis=0)
    pos_t = jnp.transpose(pos.astype(F32))
    lane = lax.broadcasted_iota(jnp.int32, (SLOTS, POSITIONS), 1).astype(F32)
    hot = []
    for image in range(IMAGES):
        row = (pos_t[:, image : image + 1] == lane).astype(F32)
        col = (pos_t[:, 2 + image : 3 + image] == lane).astype(F32)
        hot.append(jnp.concatenate([row, col], axis=1))
    hot = jnp.concatenate(hot, axis=0).astype(BF16)
    cos_sin = dot(hot, table[...].astype(BF16)).astype(BF16)

    entry = lax.broadcasted_iota(jnp.int32, (8, WIDTH), 1) % HEAD_DIM
    within = entry % HALF
    own = jnp.broadcast_to(probe[...].astype(F32), (8, WIDTH))
    after = pltpu.roll(own, WIDTH - QUARTER, 1)
    before = pltpu.roll(own, QUARTER, 1)
    partner = jnp.where(within < QUARTER, after, -before)
    key = (entry // HALF) * QUARTER + within % QUARTER
    match = lax.broadcasted_iota(jnp.int32, (GROUP, WIDTH), 0) == key[:1]
    spread_cos = jnp.where(match, own[:1], 0.0)
    spread_sin = jnp.where(match, partner[:1], 0.0)
    spread = jnp.concatenate(
        [spread_cos, spread_sin, spread_cos, spread_sin,
         jnp.zeros((2 * POSITIONS - 4 * GROUP, WIDTH), F32)],
        axis=0,
    ).astype(BF16)

    head = lax.broadcasted_iota(jnp.int32, (HEADS, WIDTH), 0) * HEAD_DIM
    column = lax.broadcasted_iota(jnp.int32, (HEADS, WIDTH), 1)
    in_head = (column >= head) & (column < head + HEAD_DIM)
    head_rows = in_head.astype(F32).astype(BF16)

    copies[0].wait()
    copies[1].wait()
    scores = jnp.zeros((HEADS, IMAGES * SLOTS), F32)
    for n, (lo, hi) in enumerate(CHUNKS):
        key_copies[n].wait()
        keys = dot(patches[...], w_key[:, lo:hi])
        turned = keys * dot(cos_sin, spread[:, lo:hi])
        high, low = split(turned)
        rows = head_rows[:, lo:hi]
        scores += dot(rows, high, 1, 1) + dot(rows, low, 1, 1)
    scores *= HEAD_DIM ** (-0.5)

    slot = lax.broadcasted_iota(jnp.int32, (HEADS, SLOTS), 1)
    sums, totals = [], []
    for image in range(IMAGES):
        live = slot < counts[image]
        part = jnp.where(live, scores[:, image * SLOTS : (image + 1) * SLOTS], MASK_FILL)
        top = jnp.max(part, axis=1, keepdims=True)
        raised = jnp.where(live, jnp.exp(part - top), 0.0)
        totals.append(jnp.sum(raised, axis=1, keepdims=True))
        sums.append(dot(raised.astype(BF16), patches[pl.ds(image * SLOTS, SLOTS)]))
    high, low = split(jnp.concatenate(sums, axis=0))
    val_copy.wait()
    acc = dot(jnp.concatenate([high, low], axis=0), w_val[...])
    acc = acc[: IMAGES * HEADS] + acc[IMAGES * HEADS :]
    pooled = [
        jnp.sum(
            jnp.where(in_head, acc[image * HEADS : (image + 1) * HEADS] / totals[image], 0.0),
            axis=0,
            keepdims=True,
        )
        for image in range(IMAGES)
    ]
    text = texts[...].astype(F32)
    first = lax.axis_index("seq") == 0
    text = jnp.concatenate(
        [jnp.where(first, text, 0.0), jnp.where(first, 0.0, text)], axis=1
    )
    message = jnp.concatenate(pooled + [text, jnp.zeros((2, WIDTH), F32)], axis=0).astype(BF16)
    for peer in range(out.shape[0]):
        out[peer] = message


def pair_kernel(gathered, w_out, txt_grad, partial, pair_rows, pooled_rows):
    members = gathered.shape[0]
    images = IMAGES * members
    loops = members // 2
    own_rows = images // loops
    half = WIDTH // 2
    loop_index = lax.axis_index("loop")
    first = lax.axis_index("seq") == 0

    block = gathered[...].astype(F32).reshape(members * 8, WIDTH).astype(BF16)
    row = lax.broadcasted_iota(jnp.int32, (images, members * 8), 0)
    source = lax.broadcasted_iota(jnp.int32, (images, members * 8), 1)
    pick_image = source == (row // IMAGES) * 8 + row % IMAGES
    text_source = (row // own_rows) * 16 + 2 + row % own_rows
    pick_text = (source == text_source) | (source == text_source + 8)
    pick = jnp.concatenate([pick_image.astype(F32), pick_text.astype(F32)], axis=0).astype(BF16)
    compact = dot(pick, block)
    pooled_f32 = compact[:images]
    pooled = pooled_f32.astype(BF16)
    texts = compact[images:].astype(BF16)
    pooled_rows[:WIDTH] = jnp.transpose(pooled_f32)
    pooled_rows[WIDTH:] = jnp.zeros((pooled_rows.shape[0] - WIDTH, images), F32)

    projected = dot(pooled, w_out[...])
    length = jnp.sqrt(jnp.sum(projected * projected, axis=1, keepdims=True) + 1e-06)
    unit = projected / length
    embedded = unit.astype(BF16)
    logit = LOGIT_SCALE * dot(embedded, texts, 1, 1) + LOGIT_BIAS
    same = lax.broadcasted_iota(jnp.int32, (images, images), 0) == lax.broadcasted_iota(
        jnp.int32, (images, images), 1
    )
    labels = jnp.where(same, 1.0, -1.0)
    pair_grad = (LOGIT_SCALE * (-labels * jax.nn.sigmoid(-labels * logit))).astype(BF16)
    image_grad = dot(pair_grad, texts)
    inner = jnp.sum(unit * image_grad, axis=1, keepdims=True)
    out_grad = ((image_grad - unit * inner) / length).astype(F32)
    out_half = jnp.where(first, out_grad[:, :half], out_grad[:, half:]).astype(BF16)

    stride = loops * 9
    rows = jnp.concatenate(
        [
            pooled_rows[pl.ds(stride * rep + 9 * loop_index, PAD_ROWS), :]
            for rep in range(partial.shape[0])
        ],
        axis=0,
    ).astype(BF16)
    partial[...] = dot(rows, out_half).astype(BF16).reshape(partial.shape)

    pair_rows[:images] = jnp.transpose(pair_grad.astype(F32))
    pair_rows[images:] = jnp.zeros((pair_rows.shape[0] - images, images), F32)
    own = dot(pair_rows[pl.ds(own_rows * loop_index, 8), :].astype(BF16), embedded)
    txt_grad[...] = jnp.where(first, own[:own_rows, :half], own[:own_rows, half:])


def local(reps, members, patches, positions, counts, probe, w_keyval, w_out, texts):
    vmem = pl.BlockSpec(memory_space=pltpu.VMEM)
    smem = pl.BlockSpec(memory_space=pltpu.SMEM)
    hbm = pl.BlockSpec(memory_space=pltpu.HBM)
    message = pl.pallas_call(
        pool_kernel,
        name="pool",
        out_shape=jax.ShapeDtypeStruct((members, 8, WIDTH), BF16),
        in_specs=[smem, vmem, vmem, vmem, vmem, hbm, hbm],
        out_specs=vmem,
        scratch_shapes=[
            pltpu.VMEM((IMAGES * SLOTS, WIDTH), BF16),
            pltpu.VMEM((WIDTH, WIDTH), BF16),
            pltpu.VMEM((WIDTH, WIDTH), BF16),
            pltpu.SemaphoreType.DMA((IMAGES,)),
            pltpu.SemaphoreType.DMA((len(CHUNKS),)),
            pltpu.SemaphoreType.DMA,
        ],
        compiler_params=pltpu.CompilerParams(vmem_limit_bytes=40 * 1024 * 1024),
    )(counts, positions, probe.reshape(1, WIDTH), jnp.asarray(angle_table()), texts, patches, w_keyval)
    gathered = lax.all_to_all(message, ("loop", "seq"), split_axis=0, concat_axis=0, tiled=True)
    images = IMAGES * members
    txt_grad, partial = pl.pallas_call(
        pair_kernel,
        name="pairs",
        out_shape=(
            jax.ShapeDtypeStruct(texts.shape, F32),
            jax.ShapeDtypeStruct((reps, PAD_ROWS, WIDTH // 2), BF16),
        ),
        in_specs=[vmem, vmem],
        out_specs=(vmem, vmem),
        scratch_shapes=[
            pltpu.VMEM((images + 8, images), F32),
            pltpu.VMEM((WIDTH + 16, images), F32),
        ],
        compiler_params=pltpu.CompilerParams(vmem_limit_bytes=24 * 1024 * 1024),
    )(gathered, w_out)
    blocks = lax.all_to_all(partial, "rep", split_axis=0, concat_axis=0, tiled=True)
    wo_grad = jnp.sum(blocks.astype(F32), axis=0)[:9]
    return (txt_grad, wo_grad)


def solution(mesh):
    reps = mesh.shape["rep"]
    members = mesh.shape["loop"] * mesh.shape["seq"]
    return jax.shard_map(
        functools.partial(local, reps, members),
        mesh=mesh,
        in_specs=(
            P(("rep", "loop", "seq"), None, None),
            P(None, ("rep", "loop", "seq"), None),
            P(("rep", "loop", "seq")),
            P(),
            P(),
            P(),
            P(("rep", "loop"), "seq"),
        ),
        out_specs=(P(("rep", "loop"), "seq"), P(("rep", "loop"), "seq")),
        check_vma=False,
    )
```

time: 859 us -> 56.4 us (0.07)
  blocking collectives: 725 us -> 37.5 us
  waiting for transfers between devices: 72.6 us -> 0 us
  matrix products: 15.9 us -> 0 us
  between operations: 14.9 us -> 0.65 us
  local copies, waits for them, and re-layouts: 20.1 us -> 7.45 us
  Pallas kernels: 0 us -> 9.81 us
    unnamed x1 -> x0, blocking collectives: 681 us -> none
    psum x8 -> x0, blocking collectives: 39.4 us -> none  [turn(): inner_sum = lax.psum(inner_rows(emb_half, text_block), 'seq')]
    all_to_all x0 -> x2, blocking collectives: none -> 37.5 us  [the longest x1 23.8 us: local(): lax.all_to_all(partial, 'rep', split_axis=0, concat_axis=0, tiled=True)]
    unnamed x2 -> x0, waiting for transfers between devices: 37.2 us -> none
    ppermute x16 -> x0, waiting for transfers between devices: 32.9 us -> none  [shifted(): return lax.ppermute(value, axis, pairs)]
    dot_general x28 -> x0, matrix products: 15.9 us -> none  [the longest x1 6.23 us: local(): jnp.dot(patches.reshape(images * slots, width), w_keyval, preferred_eleme...]
    pallas_call x0 -> x2, Pallas kernels: none -> 9.81 us  [the longest x1 7.68 us: local(): pl.pallas_call(pool_kernel, name='pool', out_shape=jax.ShapeDtypeStruct((...]
  transfers between devices with their start and end apart: 18 -> 0, of which waited for: 10 -> 0; matrix products, arithmetic and copies ran while one was open for 0% -> 0% of each run, Pallas kernels for 0% -> 0%
where the time goes in v1:
time: 56.4 us; the launch traced here: 56.1 us
  blocking collectives  37.5 us (66%)
  Pallas kernels  9.81 us (17%)
  local copies, waits for them, and re-layouts  7.45 us (13%)
  other arithmetic  0.67 us (1%)
  between operations  0.65 us (1%)
    all_to_all x1, blocking collectives, local(): lax.all_to_all(partial, 'rep', split_axis=0, concat_axis=0, tiled=True)  23.8 us
    all_to_all x1, blocking collectives, local(): lax.all_to_all(message, ('loop', 'seq'), split_axis=0, concat_axis=0, til...  13.7 us
    pallas_call x1, Pallas kernels, local(): pl.pallas_call(pool_kernel, name='pool', out_shape=jax.ShapeDtypeStruct((...  7.68 us
    unnamed x14, local copies, waits for them, and re-layouts  6.76 us
    pallas_call x1, Pallas kernels, local(): pl.pallas_call(pair_kernel, name='pairs', out_shape=(jax.ShapeDtypeStruct...  2.13 us

profile of v1, /device:TPU:32, one launch (start us, length us, event | category | flops | bytes accessed | tf_op | source)
XLA Modules:
  0.0 56.1 jit_solution(5238715888605597842)
XLA Ops:
  0.6 0.7 %reshape.7.probe = bf16[1,1152]{1,0:T(2,128)(2,1)S(1)} reshape(bf16[1152]{0:T(1024)(128)(2,1)} %param.11) | data formatting | bytes 4608 | tf_op jit(solution)/shard_map/reshape | solution.py:231
  1.3 0.0 copy-start
  1.3 2.5 %copy-done = bf16[1152,2304]{1,0:T(8,128)(2,1)S(1)} copy-done((bf16[1152,2304]{1,0:T(8,128)(2,1)S(1)}, bf16[1152,2304]{1,0:T(8,128)(2,1)}, u32[]{:S(2)}) %copy-start) | copy-done | bytes 5308440
  3.8 0.0 copy-start.2
  3.8 1.3 %copy-done.2 = bf16[2,256,1152]{2,1,0:T(8,128)(2,1)S(1)} copy-done((bf16[2,256,1152]{2,1,0:T(8,128)(2,1)S(1)}, bf16[2,256,1152]{2,1,0:T(8,128)(2,1)}, u32[]{:S(2)}) %copy-start.2) | copy-done | bytes 1179672
  5.1 0.0 copy-start.3
  5.1 0.9 %copy-done.3 = f32[256,256]{1,0:T(8,128)S(1)} copy-done((f32[256,256]{1,0:T(8,128)S(1)}, f32[256,256]{1,0:T(8,128)}, u32[]{:S(2)}) %copy-start.3) | copy-done | bytes 262168
  6.0 0.0 copy-start.4
  6.1 0.7 %copy-done.4 = bf16[4,576]{1,0:T(4,128)(2,1)S(1)} copy-done((bf16[4,576]{1,0:T(4,128)(2,1)S(1)}, bf16[4,576]{1,0:T(4,128)(2,1)}, u32[]{:S(2)}) %copy-start.4) | copy-done | bytes 4632
  6.7 0.0 copy-start.5
  6.7 0.7 %copy-done.5 = s32[2,2,256]{2,1,0:T(2,128)S(1)} copy-done((s32[2,2,256]{2,1,0:T(2,128)S(1)}, s32[2,2,256]{2,1,0:T(2,128)}, u32[]{:S(2)}) %copy-start.5) | copy-done | bytes 4120
  7.4 0.0 copy-start.6
  7.4 0.7 %copy-done.6 = s32[2]{0:T(128)S(1)} copy-done((s32[2]{0:T(128)S(1)}, s32[2]{0:T(128)}, u32[]{:S(2)}) %copy-start.6) | copy-done | bytes 32
  8.1 0.0 copy-start.1
  8.1 7.7 %pool.1 = bf16[16,8,1152]{2,1,0:T(8,128)(2,1)S(1)} custom-call(s32[2]{0:T(128)S(1)} %copy-done.6, s32[2,2,256]{2,1,0:T(2,128)S(1)} %copy-done.5, bf16[1,1152]{1,0:T(2,128)(2,1)S(1)} %reshape.7.probe, f32[256,256]{1,0:T(8,128)S(1)} %copy-done.3, bf16[4,576]{1,0:T(4,128)(2,1)S(1)} %copy-done.4, bf16[2,256,1152]{2,1,0:T(8,128)(2,1)S(1)} %copy-done.2, ...), custom_call_target="tpu_custom_call" | custom-call | tf_op jit(solution)/shard_map/pool/pallas_call | solution.py:216
  15.8 13.7 %all_to_all.10.gathered = bf16[16,8,1152]{2,1,0:T(8,128)(2,1)S(1)} all-to-all(bf16[16,8,1152]{2,1,0:T(8,128)(2,1)S(1)} %pool.1), channel_id=1, replica_groups=mesh['rep'=16,'loop'=8,'seq'=2] {'loop','seq'}, dimensions={0} | all-to-all | bytes 589824 | tf_op jit(solution)/shard_map/all_to_all | solution.py:232
  29.5 0.0 copy-done.1
  29.5 2.1 %pairs.1 = (f32[4,576]{1,0:T(4,128)}, bf16[16,16,576]{2,1,0:T(8,128)(2,1)S(1)}) custom-call(bf16[16,8,1152]{2,1,0:T(8,128)(2,1)S(1)} %all_to_all.10.gathered, bf16[1152,1152]{1,0:T(8,128)(2,1)S(1)} %copy-done.1), custom_call_target="tpu_custom_call" | custom-call | tf_op jit(solution)/shard_map/pairs/pallas_call | solution.py:234
  31.6 23.8 %all_to_all.11 = bf16[16,16,576]{2,1,0:T(8,128)(2,1)S(1)} all-to-all(bf16[16,16,576]{2,1,0:T(8,128)(2,1)S(1)} %get-tuple-element.5), channel_id=1, replica_groups=mesh['rep'=16,'loop'=8,'seq'=2] {'rep'}, dimensions={0} | all-to-all | bytes 589824 | tf_op jit(solution)/shard_map/all_to_all | solution.py:249
  55.4 0.7 %convert_reduce_fusion = f32[16,576]{1,0:T(8,128)} fusion(bf16[16,16,576]{2,1,0:T(8,128)(2,1)S(1)} %all_to_all.11), kind=kLoop, calls=%fused_computation | loop fusion | flops 285696 | bytes 331776 | tf_op jit(solution)/shard_map/reduce_sum | solution.py:250
Async XLA Ops:
  1.3 2.5 %copy-start = (bf16[1152,2304]{1,0:T(8,128)(2,1)S(1)}, bf16[1152,2304]{1,0:T(8,128)(2,1)}, u32[]{:S(2)}) copy-start(bf16[1152,2304]{1,0:T(8,128)(2,1)} %weights_hbm.1) | copy-start | bytes 15925252
  3.8 1.3 %copy-start.2 = (bf16[2,256,1152]{2,1,0:T(8,128)(2,1)S(1)}, bf16[2,256,1152]{2,1,0:T(8,128)(2,1)}, u32[]{:S(2)}) copy-start(bf16[2,256,1152]{2,1,0:T(8,128)(2,1)} %patches_hbm.1) | copy-start | bytes 3538948
  5.1 0.9 %copy-start.3 = (f32[256,256]{1,0:T(8,128)S(1)}, f32[256,256]{1,0:T(8,128)}, u32[]{:S(2)}) copy-start(f32[256,256]{1,0:T(8,128)} %constant.4.clone.table) | copy-start | bytes 786436
  6.0 0.7 %copy-start.4 = (bf16[4,576]{1,0:T(4,128)(2,1)S(1)}, bf16[4,576]{1,0:T(4,128)(2,1)}, u32[]{:S(2)}) copy-start(bf16[4,576]{1,0:T(4,128)(2,1)} %texts.1) | copy-start | bytes 13828
  6.7 0.7 %copy-start.5 = (s32[2,2,256]{2,1,0:T(2,128)S(1)}, s32[2,2,256]{2,1,0:T(2,128)}, u32[]{:S(2)}) copy-start(s32[2,2,256]{2,1,0:T(2,128)} %positions.1) | copy-start | bytes 12292
  7.4 0.7 %copy-start.6 = (s32[2]{0:T(128)S(1)}, s32[2]{0:T(128)}, u32[]{:S(2)}) copy-start(s32[2]{0:T(128)} %counts.1) | copy-start | bytes 28
  8.1 21.4 %copy-start.1 = (bf16[1152,1152]{1,0:T(8,128)(2,1)S(1)}, bf16[1152,1152]{1,0:T(8,128)(2,1)}, u32[]{:S(2)}) copy-start(bf16[1152,1152]{1,0:T(8,128)(2,1)} %w_out.1) | copy-start | bytes 7962628

commit v2 on v1

--- a/solution.py
+++ b/solution.py
@@ -22,7 +22,6 @@
 LOGIT_BIAS = -2.0
 
 GROUP = 40
-CHUNKS = ((0, 256), (256, 512), (512, 768), (768, 1024), (1024, 1152))
 PAD_ROWS = 16
 
 BF16 = jnp.bfloat16
@@ -54,31 +53,38 @@
 
 
 def pool_kernel(
-    counts, positions, probe, table, texts, patches_hbm, weights_hbm, out,
-    patches, w_key, w_val, patch_sem, key_sem, val_sem,
+    counts_hbm, positions_hbm, probe_hbm, table_hbm, texts_hbm, patches_hbm, weights_hbm, out,
+    counts, positions, probe, table, texts, patches, w_key, w_val,
+    small_sem, patch_sem, key_sem, val_sem,
 ):
-    copies = []
-    for image in range(IMAGES):
-        copies.append(
-            pltpu.make_async_copy(
-                patches_hbm.at[image],
-                patches.at[pl.ds(image * SLOTS, SLOTS)],
-                patch_sem.at[image],
+    small = [
+        pltpu.make_async_copy(source, target, small_sem.at[n])
+        for n, (source, target) in enumerate(
+            (
+                (positions_hbm, positions),
+                (table_hbm, table),
+                (probe_hbm, probe),
+                (texts_hbm, texts),
+                (counts_hbm, counts),
             )
         )
-    key_copies = [
+    ]
+    copies = [
         pltpu.make_async_copy(
-            weights_hbm.at[:, pl.ds(lo, hi - lo)], w_key.at[:, pl.ds(lo, hi - lo)], key_sem.at[n]
+            patches_hbm.at[image],
+            patches.at[pl.ds(image * SLOTS, SLOTS)],
+            patch_sem.at[image],
         )
-        for n, (lo, hi) in enumerate(CHUNKS)
-    ]
+        for image in range(IMAGES)
+    ]
+    copies.append(
+        pltpu.make_async_copy(weights_hbm.at[:, pl.ds(0, WIDTH)], w_key, key_sem)
+    )
     val_copy = pltpu.make_async_copy(weights_hbm.at[:, pl.ds(WIDTH, WIDTH)], w_val, val_sem)
-    copies[0].start()
-    key_copies[0].start()
-    copies[1].start()
-    for copy in key_copies[1:]:
+    for copy in small + copies + [val_copy]:
         copy.start()
-    val_copy.start()
+    for copy in small:
+        copy.wait()
 
     pos = jnp.concatenate([positions[0], positions[1], jnp.zeros((4, SLOTS), jnp.int32)], axis=0)
     pos_t = jnp.transpose(pos.astype(F32))
@@ -93,7 +99,7 @@
 
     entry = lax.broadcasted_iota(jnp.int32, (8, WIDTH), 1) % HEAD_DIM
     within = entry % HALF
-    own = jnp.broadcast_to(probe[...].astype(F32), (8, WIDTH))
+    own = jnp.broadcast_to(probe[...].astype(F32).reshape(1, WIDTH), (8, WIDTH))
     after = pltpu.roll(own, WIDTH - QUARTER, 1)
     before = pltpu.roll(own, QUARTER, 1)
     partner = jnp.where(within < QUARTER, after, -before)
@@ -110,19 +116,17 @@
     head = lax.broadcasted_iota(jnp.int32, (HEADS, WIDTH), 0) * HEAD_DIM
     column = lax.broadcasted_iota(jnp.int32, (HEADS, WIDTH), 1)
     in_head = (column >= head) & (column < head + HEAD_DIM)
-    head_rows = in_head.astype(F32).astype(BF16)
-
-    copies[0].wait()
-    copies[1].wait()
-    scores = jnp.zeros((HEADS, IMAGES * SLOTS), F32)
-    for n, (lo, hi) in enumerate(CHUNKS):
-        key_copies[n].wait()
-        keys = dot(patches[...], w_key[:, lo:hi])
-        turned = keys * dot(cos_sin, spread[:, lo:hi])
-        high, low = split(turned)
-        rows = head_rows[:, lo:hi]
-        scores += dot(rows, high, 1, 1) + dot(rows, low, 1, 1)
-    scores *= HEAD_DIM ** (-0.5)
+
+    head_row = lax.broadcasted_iota(jnp.int32, (WIDTH, HEADS), 0)
+    head_lane = lax.broadcasted_iota(jnp.int32, (WIDTH, HEADS), 1) * HEAD_DIM
+    head_cols = (head_row >= head_lane) & (head_row < head_lane + HEAD_DIM)
+    head_cols = head_cols.astype(F32).astype(BF16)
+
+    for copy in copies:
+        copy.wait()
+    keys = dot(patches[...], w_key[...])
+    high, low = split(keys * dot(cos_sin, spread))
+    scores = jnp.transpose(dot(high, head_cols) + dot(low, head_cols)) * HEAD_DIM ** (-0.5)
 
     slot = lax.broadcasted_iota(jnp.int32, (HEADS, SLOTS), 1)
     sums, totals = [], []
@@ -146,11 +150,11 @@
         for image in range(IMAGES)
     ]
     text = texts[...].astype(F32)
-    first = lax.axis_index("seq") == 0
-    text = jnp.concatenate(
-        [jnp.where(first, text, 0.0), jnp.where(first, 0.0, text)], axis=1
-    )
-    message = jnp.concatenate(pooled + [text, jnp.zeros((2, WIDTH), F32)], axis=0).astype(BF16)
+    pairs = [
+        jnp.concatenate([text[n : n + 1], text[n + 1 : n + 2]], axis=1)
+        for n in range(0, texts.shape[0], 2)
+    ]
+    message = jnp.concatenate(pooled + pairs, axis=0).astype(BF16)
     for peer in range(out.shape[0]):
         out[peer] = message
 
@@ -164,17 +168,23 @@
     loop_index = lax.axis_index("loop")
     first = lax.axis_index("seq") == 0
 
-    block = gathered[...].astype(F32).reshape(members * 8, WIDTH).astype(BF16)
-    row = lax.broadcasted_iota(jnp.int32, (images, members * 8), 0)
-    source = lax.broadcasted_iota(jnp.int32, (images, members * 8), 1)
-    pick_image = source == (row // IMAGES) * 8 + row % IMAGES
-    text_source = (row // own_rows) * 16 + 2 + row % own_rows
-    pick_text = (source == text_source) | (source == text_source + 8)
-    pick = jnp.concatenate([pick_image.astype(F32), pick_text.astype(F32)], axis=0).astype(BF16)
+    height = gathered.shape[1]
+    block = gathered[...].astype(F32).reshape(members * height, WIDTH).astype(BF16)
+    row = lax.broadcasted_iota(jnp.int32, (images, members * height), 0)
+    source = lax.broadcasted_iota(jnp.int32, (images, members * height), 1)
+    pick_image = source == (row // IMAGES) * height + row % IMAGES
+    text_source = (row // own_rows) * 2 * height + IMAGES + (row % own_rows) // 2
+    pick = [pick_image, source == text_source, source == text_source + height]
+    pick = jnp.concatenate([one.astype(F32) for one in pick], axis=0).astype(BF16)
     compact = dot(pick, block)
     pooled_f32 = compact[:images]
     pooled = pooled_f32.astype(BF16)
-    texts = compact[images:].astype(BF16)
+    even = lax.broadcasted_iota(jnp.int32, (images, half), 0) % 2 == 0
+    halves = [
+        jnp.where(even, part[:, :half], part[:, half:])
+        for part in (compact[images : 2 * images], compact[2 * images :])
+    ]
+    texts = jnp.concatenate(halves, axis=1).astype(BF16)
     pooled_rows[:WIDTH] = jnp.transpose(pooled_f32)
     pooled_rows[WIDTH:] = jnp.zeros((pooled_rows.shape[0] - WIDTH, images), F32)
 
@@ -211,24 +221,30 @@
 
 def local(reps, members, patches, positions, counts, probe, w_keyval, w_out, texts):
     vmem = pl.BlockSpec(memory_space=pltpu.VMEM)
-    smem = pl.BlockSpec(memory_space=pltpu.SMEM)
     hbm = pl.BlockSpec(memory_space=pltpu.HBM)
     message = pl.pallas_call(
         pool_kernel,
         name="pool",
-        out_shape=jax.ShapeDtypeStruct((members, 8, WIDTH), BF16),
-        in_specs=[smem, vmem, vmem, vmem, vmem, hbm, hbm],
+        out_shape=pltpu.VMEM((members, IMAGES + texts.shape[0] // 2, WIDTH), BF16),
+        in_specs=[hbm] * 7,
         out_specs=vmem,
         scratch_shapes=[
+            pltpu.SMEM((IMAGES,), jnp.int32),
+            pltpu.VMEM(positions.shape, jnp.int32),
+            pltpu.VMEM(probe.shape, BF16),
+            pltpu.VMEM((2 * POSITIONS, 2 * POSITIONS), F32),
+            pltpu.VMEM(texts.shape, BF16),
             pltpu.VMEM((IMAGES * SLOTS, WIDTH), BF16),
             pltpu.VMEM((WIDTH, WIDTH), BF16),
             pltpu.VMEM((WIDTH, WIDTH), BF16),
+            pltpu.SemaphoreType.DMA((5,)),
             pltpu.SemaphoreType.DMA((IMAGES,)),
-            pltpu.SemaphoreType.DMA((len(CHUNKS),)),
+            pltpu.SemaphoreType.DMA,
             pltpu.SemaphoreType.DMA,
         ],
-        compiler_params=pltpu.CompilerParams(vmem_limit_bytes=40 * 1024 * 1024),
-    )(counts, positions, probe.reshape(1, WIDTH), jnp.asarray(angle_table()), texts, patches, w_keyval)
+        compiler_params=pltpu.CompilerParams(vmem_limit_bytes=60 * 1024 * 1024),
+    )(counts, positions, probe, jnp.asarray(angle_table()), texts, patches, w_keyval)
+    message, w_out = lax.optimization_barrier((message, w_out))
     gathered = lax.all_to_all(message, ("loop", "seq"), split_axis=0, concat_axis=0, tiled=True)
     images = IMAGES * members
     txt_grad, partial = pl.pallas_call(

time: 56.4 us -> 45.9 us (0.81)
  local copies, waits for them, and re-layouts: 7.45 us -> 0.01 us
  blocking collectives: 37.5 us -> 36 us
  Pallas kernels: 9.81 us -> 8.43 us
    unnamed x14 -> x2, local copies, waits for them, and re-layouts: 6.76 us -> 0.01 us
    all_to_all x1, blocking collectives: 13.7 us -> 12.2 us  [local(): lax.all_to_all(message, ('loop', 'seq'), split_axis=0, concat_axis=0, til...]
    pallas_call x1, Pallas kernels: 7.68 us -> 6.27 us  [local(): pl.pallas_call(pool_kernel, name='pool', out_shape=pltpu.VMEM((members, I...]
    reshape x1 -> x0, local copies, waits for them, and re-layouts: 0.69 us -> none  [local(): probe.reshape(1, WIDTH)]
where the time goes in v2:
time: 45.9 us; the launch traced here: 45.8 us
  blocking collectives  36 us (78%)
  Pallas kernels  8.43 us (18%)
  other arithmetic  0.67 us (1%)
  between operations  0.65 us (1%)
    all_to_all x1, blocking collectives, local(): lax.all_to_all(partial, 'rep', split_axis=0, concat_axis=0, tiled=True)  23.8 us
    all_to_all x1, blocking collectives, local(): lax.all_to_all(message, ('loop', 'seq'), split_axis=0, concat_axis=0, til...  12.2 us
    pallas_call x1, Pallas kernels, local(): pl.pallas_call(pool_kernel, name='pool', out_shape=pltpu.VMEM((members, I...  6.27 us
    pallas_call x1, Pallas kernels, local(): pl.pallas_call(pair_kernel, name='pairs', out_shape=(jax.ShapeDtypeStruct...  2.16 us

profile of v2, /device:TPU:32, one launch (start us, length us, event | category | flops | bytes accessed | tf_op | source)
XLA Modules:
  0.0 45.8 jit_solution(14736569460515931501)
XLA Ops:
  0.6 0.0 copy-start
  0.6 6.3 %pool.1 = bf16[16,4,1152]{2,1,0:T(4,128)(2,1)S(1)} custom-call(s32[2]{0:T(128)} %counts_hbm.1, s32[2,2,256]{2,1,0:T(2,128)} %positions_hbm.1, bf16[1152]{0:T(1024)(128)(2,1)} %probe_hbm.1, f32[256,256]{1,0:T(8,128)} %constant.4.clone.table_hbm, bf16[4,576]{1,0:T(4,128)(2,1)} %texts_hbm.1, bf16[2,256,1152]{2,1,0:T(8,128)(2,1)} %patches_hbm.1, ...), custom_call_target="tpu_custom_call" | custom-call | tf_op jit(solution)/shard_map/pool/pallas_call | solution.py:225
  6.9 12.2 %all_to_all.10.gathered = bf16[16,4,1152]{2,1,0:T(4,128)(2,1)S(1)} all-to-all(bf16[16,4,1152]{2,1,0:T(4,128)(2,1)S(1)} %pool.1), channel_id=1, replica_groups=mesh['rep'=16,'loop'=8,'seq'=2] {'loop','seq'}, dimensions={0} | all-to-all | bytes 294912 | tf_op jit(solution)/shard_map/all_to_all | solution.py:248
  19.2 0.0 copy-done
  19.2 2.2 %pairs.1 = (f32[4,576]{1,0:T(4,128)}, bf16[16,16,576]{2,1,0:T(8,128)(2,1)S(1)}) custom-call(bf16[16,4,1152]{2,1,0:T(4,128)(2,1)S(1)} %all_to_all.10.gathered, bf16[1152,1152]{1,0:T(8,128)(2,1)S(1)} %copy-done), custom_call_target="tpu_custom_call" | custom-call | tf_op jit(solution)/shard_map/pairs/pallas_call | solution.py:250
  21.3 23.8 %all_to_all.11 = bf16[16,16,576]{2,1,0:T(8,128)(2,1)S(1)} all-to-all(bf16[16,16,576]{2,1,0:T(8,128)(2,1)S(1)} %get-tuple-element.9), channel_id=1, replica_groups=mesh['rep'=16,'loop'=8,'seq'=2] {'rep'}, dimensions={0} | all-to-all | bytes 589824 | tf_op jit(solution)/shard_map/all_to_all | solution.py:265
  45.1 0.7 %convert_reduce_fusion = f32[16,576]{1,0:T(8,128)} fusion(bf16[16,16,576]{2,1,0:T(8,128)(2,1)S(1)} %all_to_all.11), kind=kLoop, calls=%fused_computation | loop fusion | flops 285696 | bytes 331776 | tf_op jit(solution)/shard_map/reduce_sum | solution.py:266
Async XLA Ops:
  0.6 18.5 %copy-start = (bf16[1152,1152]{1,0:T(8,128)(2,1)S(1)}, bf16[1152,1152]{1,0:T(8,128)(2,1)}, u32[]{:S(2)}) copy-start(bf16[1152,1152]{1,0:T(8,128)(2,1)} %w_out) | copy-start | bytes 7962628

commit v3 on v2

--- a/solution.py
+++ b/solution.py
@@ -22,7 +22,10 @@
 LOGIT_BIAS = -2.0
 
 GROUP = 40
-PAD_ROWS = 16
+OWN_ROWS = 9
+FOLD = 8
+FOLD_AT = 640
+MESSAGE = 768
 
 BF16 = jnp.bfloat16
 F32 = jnp.float32
@@ -159,7 +162,7 @@
         out[peer] = message
 
 
-def pair_kernel(gathered, w_out, txt_grad, partial, pair_rows, pooled_rows):
+def pair_kernel(gathered, w_out, txt_grad, partial, pair_rows, pooled_rows, folded):
     members = gathered.shape[0]
     images = IMAGES * members
     loops = members // 2
@@ -203,20 +206,37 @@
     out_grad = ((image_grad - unit * inner) / length).astype(F32)
     out_half = jnp.where(first, out_grad[:, :half], out_grad[:, half:]).astype(BF16)
 
-    stride = loops * 9
+    reps = partial.shape[0]
+    stride = loops * OWN_ROWS
+    start = OWN_ROWS * loop_index
     rows = jnp.concatenate(
-        [
-            pooled_rows[pl.ds(stride * rep + 9 * loop_index, PAD_ROWS), :]
-            for rep in range(partial.shape[0])
-        ],
+        [pooled_rows[pl.ds(stride * rep + start, FOLD), :] for rep in range(reps)]
+        + [pooled_rows[pl.ds(stride * rep + start + FOLD, 1), :] for rep in range(reps)],
         axis=0,
     ).astype(BF16)
-    partial[...] = dot(rows, out_half).astype(BF16).reshape(partial.shape)
+    padded = jnp.concatenate([out_half, jnp.zeros((images, FOLD_AT - half), BF16)], axis=1)
+    sums = dot(rows, padded)
+    partial[:, :, :FOLD_AT] = sums[: reps * FOLD].reshape(reps, FOLD, FOLD_AT).astype(BF16)
+    width = half // FOLD
+    folded[...] = jnp.zeros(folded.shape, F32)
+    for n in range(FOLD):
+        folded[pl.ds(n, reps, FOLD), :width] = sums[reps * FOLD :, n * width : (n + 1) * width]
+    partial[:, :, FOLD_AT:] = folded[...].reshape(reps, FOLD, MESSAGE - FOLD_AT).astype(BF16)
 
     pair_rows[:images] = jnp.transpose(pair_grad.astype(F32))
     pair_rows[images:] = jnp.zeros((pair_rows.shape[0] - images, images), F32)
     own = dot(pair_rows[pl.ds(own_rows * loop_index, 8), :].astype(BF16), embedded)
     txt_grad[...] = jnp.where(first, own[:own_rows, :half], own[:own_rows, half:])
+
+
+def sum_kernel(blocks, out):
+    total = jnp.sum(blocks[...].astype(F32), axis=0)
+    half = out.shape[1]
+    width = half // FOLD
+    out[:FOLD] = total[:, :half]
+    out[FOLD:] = jnp.concatenate(
+        [total[n : n + 1, FOLD_AT : FOLD_AT + width] for n in range(FOLD)], axis=1
+    )
 
 
 def local(reps, members, patches, positions, counts, probe, w_keyval, w_out, texts):
@@ -252,18 +272,25 @@
         name="pairs",
         out_shape=(
             jax.ShapeDtypeStruct(texts.shape, F32),
-            jax.ShapeDtypeStruct((reps, PAD_ROWS, WIDTH // 2), BF16),
+            jax.ShapeDtypeStruct((reps, FOLD, MESSAGE), BF16),
         ),
         in_specs=[vmem, vmem],
         out_specs=(vmem, vmem),
         scratch_shapes=[
             pltpu.VMEM((images + 8, images), F32),
             pltpu.VMEM((WIDTH + 16, images), F32),
+            pltpu.VMEM((reps * FOLD, MESSAGE - FOLD_AT), F32),
         ],
         compiler_params=pltpu.CompilerParams(vmem_limit_bytes=24 * 1024 * 1024),
     )(gathered, w_out)
     blocks = lax.all_to_all(partial, "rep", split_axis=0, concat_axis=0, tiled=True)
-    wo_grad = jnp.sum(blocks.astype(F32), axis=0)[:9]
+    wo_grad = pl.pallas_call(
+        sum_kernel,
+        name="sums",
+        out_shape=jax.ShapeDtypeStruct((OWN_ROWS, WIDTH // 2), F32),
+        in_specs=[vmem],
+        out_specs=vmem,
+    )(blocks)
     return (txt_grad, wo_grad)
 
 

time: 45.9 us -> 44.6 us (0.972)
  blocking collectives: 36 us -> 33.7 us
  Pallas kernels: 8.43 us -> 10.1 us
  other arithmetic: 0.67 us -> 0 us
    all_to_all x1, blocking collectives: 23.8 us -> 21.5 us  [local(): lax.all_to_all(partial, 'rep', split_axis=0, concat_axis=0, tiled=True)]
    pallas_call x0 -> x1, Pallas kernels: none -> 1.64 us  [local(): pl.pallas_call(sum_kernel, name='sums', out_shape=jax.ShapeDtypeStruct((O...]
    reduce_sum x1 -> x0, other arithmetic: 0.67 us -> none  [local(): wo_grad = jnp.sum(blocks.astype(F32), axis=0)[:9]]
where the time goes in v3:
time: 44.6 us; the launch traced here: 44.4 us
  blocking collectives  33.7 us (76%)
  Pallas kernels  10.1 us (23%)
  between operations  0.65 us (1%)
    all_to_all x1, blocking collectives, local(): lax.all_to_all(partial, 'rep', split_axis=0, concat_axis=0, tiled=True)  21.5 us
    all_to_all x1, blocking collectives, local(): lax.all_to_all(message, ('loop', 'seq'), split_axis=0, concat_axis=0, til...  12.2 us
    pallas_call x1, Pallas kernels, local(): pl.pallas_call(pool_kernel, name='pool', out_shape=pltpu.VMEM((members, I...  6.27 us
    pallas_call x1, Pallas kernels, local(): pl.pallas_call(pair_kernel, name='pairs', out_shape=(jax.ShapeDtypeStruct...  2.15 us
    pallas_call x1, Pallas kernels, local(): pl.pallas_call(sum_kernel, name='sums', out_shape=jax.ShapeDtypeStruct((O...  1.64 us

profile of v3, /device:TPU:32, one launch (start us, length us, event | category | flops | bytes accessed | tf_op | source)
XLA Modules:
  0.0 44.4 jit_solution(9490587065332560781)
XLA Ops:
  0.6 0.0 copy-start
  0.6 6.3 %pool.1 = bf16[16,4,1152]{2,1,0:T(4,128)(2,1)S(1)} custom-call(s32[2]{0:T(128)} %counts_hbm.1, s32[2,2,256]{2,1,0:T(2,128)} %positions_hbm.1, bf16[1152]{0:T(1024)(128)(2,1)} %probe_hbm.1, f32[256,256]{1,0:T(8,128)} %constant.2.clone.table_hbm, bf16[4,576]{1,0:T(4,128)(2,1)} %texts_hbm.1, bf16[2,256,1152]{2,1,0:T(8,128)(2,1)} %patches_hbm.1, ...), custom_call_target="tpu_custom_call" | custom-call | tf_op jit(solution)/shard_map/pool/pallas_call | solution.py:245
  6.9 12.2 %all_to_all.10.gathered = bf16[16,4,1152]{2,1,0:T(4,128)(2,1)S(1)} all-to-all(bf16[16,4,1152]{2,1,0:T(4,128)(2,1)S(1)} %pool.1), channel_id=1, replica_groups=mesh['rep'=16,'loop'=8,'seq'=2] {'loop','seq'}, dimensions={0} | all-to-all | bytes 294912 | tf_op jit(solution)/shard_map/all_to_all | solution.py:268
  19.2 0.0 copy-done
  19.2 2.1 %pairs.1 = (f32[4,576]{1,0:T(4,128)}, bf16[16,8,768]{2,1,0:T(8,128)(2,1)S(1)}) custom-call(bf16[16,4,1152]{2,1,0:T(4,128)(2,1)S(1)} %all_to_all.10.gathered, bf16[1152,1152]{1,0:T(8,128)(2,1)S(1)} %copy-done), custom_call_target="tpu_custom_call" | custom-call | tf_op jit(solution)/shard_map/pairs/pallas_call | solution.py:270
  21.3 21.5 %all_to_all.11.blocks = bf16[16,8,768]{2,1,0:T(8,128)(2,1)} all-to-all(bf16[16,8,768]{2,1,0:T(8,128)(2,1)S(1)} %get-tuple-element.9), channel_id=1, replica_groups=mesh['rep'=16,'loop'=8,'seq'=2] {'rep'}, dimensions={0} | all-to-all | bytes 393216 | tf_op jit(solution)/shard_map/all_to_all | solution.py:286
  42.8 1.6 %sums.1 = f32[9,576]{1,0:T(8,128)} custom-call(bf16[16,8,768]{2,1,0:T(8,128)(2,1)} %all_to_all.11.blocks), custom_call_target="tpu_custom_call" | custom-call | tf_op jit(solution)/shard_map/sums/pallas_call | solution.py:287
Async XLA Ops:
  0.6 18.5 %copy-start = (bf16[1152,1152]{1,0:T(8,128)(2,1)S(1)}, bf16[1152,1152]{1,0:T(8,128)(2,1)}, u32[]{:S(2)}) copy-start(bf16[1152,1152]{1,0:T(8,128)(2,1)} %w_out) | copy-start | bytes 7962628

commit v4 on v3

--- a/solution.py
+++ b/solution.py
@@ -229,7 +229,8 @@
     txt_grad[...] = jnp.where(first, own[:own_rows, :half], own[:own_rows, half:])
 
 
-def sum_kernel(blocks, out):
+def sum_kernel(blocks, text_sums, out, text_out):
+    text_out[...] = text_sums[...]
     total = jnp.sum(blocks[...].astype(F32), axis=0)
     half = out.shape[1]
     width = half // FOLD
@@ -271,8 +272,8 @@
         pair_kernel,
         name="pairs",
         out_shape=(
-            jax.ShapeDtypeStruct(texts.shape, F32),
-            jax.ShapeDtypeStruct((reps, FOLD, MESSAGE), BF16),
+            pltpu.VMEM(texts.shape, F32),
+            pltpu.VMEM((reps, FOLD, MESSAGE), BF16),
         ),
         in_specs=[vmem, vmem],
         out_specs=(vmem, vmem),
@@ -284,13 +285,17 @@
         compiler_params=pltpu.CompilerParams(vmem_limit_bytes=24 * 1024 * 1024),
     )(gathered, w_out)
     blocks = lax.all_to_all(partial, "rep", split_axis=0, concat_axis=0, tiled=True)
-    wo_grad = pl.pallas_call(
+    wo_grad, txt_grad = pl.pallas_call(
         sum_kernel,
         name="sums",
-        out_shape=jax.ShapeDtypeStruct((OWN_ROWS, WIDTH // 2), F32),
-        in_specs=[vmem],
-        out_specs=vmem,
-    )(blocks)
+        out_shape=(
+            jax.ShapeDtypeStruct((OWN_ROWS, WIDTH // 2), F32),
+            jax.ShapeDtypeStruct(texts.shape, F32),
+        ),
+        in_specs=[vmem, vmem],
+        out_specs=(vmem, vmem),
+        compiler_params=pltpu.CompilerParams(vmem_limit_bytes=16 * 1024 * 1024),
+    )(blocks, txt_grad)
     return (txt_grad, wo_grad)
 
 

time: 44.6 us -> 42.9 us (0.962)
  Pallas kernels: 10.1 us -> 8.53 us
    pallas_call x2, Pallas kernels: 3.79 us -> 2.26 us  [the longest x1 1.54 us: local(): pl.pallas_call(pair_kernel, name='pairs', out_shape=(pltpu.VMEM(texts.sha...]
where the time goes in v4:
time: 42.9 us; the launch traced here: 42.8 us
  blocking collectives  33.6 us (78%)
  Pallas kernels  8.53 us (20%)
  between operations  0.66 us (2%)
    all_to_all x1, blocking collectives, local(): lax.all_to_all(partial, 'rep', split_axis=0, concat_axis=0, tiled=True)  21.4 us
    all_to_all x1, blocking collectives, local(): lax.all_to_all(message, ('loop', 'seq'), split_axis=0, concat_axis=0, til...  12.2 us
    pallas_call x1, Pallas kernels, local(): pl.pallas_call(pool_kernel, name='pool', out_shape=pltpu.VMEM((members, I...  6.27 us
    pallas_call x1, Pallas kernels, local(): pl.pallas_call(pair_kernel, name='pairs', out_shape=(pltpu.VMEM(texts.sha...  1.54 us

profile of v4, /device:TPU:32, one launch (start us, length us, event | category | flops | bytes accessed | tf_op | source)
XLA Modules:
  0.0 42.8 jit_solution(10889600668809631858)
XLA Ops:
  0.6 0.0 copy-start
  0.6 6.3 %pool.1 = bf16[16,4,1152]{2,1,0:T(4,128)(2,1)S(1)} custom-call(s32[2]{0:T(128)} %counts_hbm.1, s32[2,2,256]{2,1,0:T(2,128)} %positions_hbm.1, bf16[1152]{0:T(1024)(128)(2,1)} %probe_hbm.1, f32[256,256]{1,0:T(8,128)} %constant.2.clone.table_hbm, bf16[4,576]{1,0:T(4,128)(2,1)} %texts_hbm.1, bf16[2,256,1152]{2,1,0:T(8,128)(2,1)} %patches_hbm.1, ...), custom_call_target="tpu_custom_call" | custom-call | tf_op jit(solution)/shard_map/pool/pallas_call | solution.py:246
  6.9 12.2 %all_to_all.10.gathered = bf16[16,4,1152]{2,1,0:T(4,128)(2,1)S(1)} all-to-all(bf16[16,4,1152]{2,1,0:T(4,128)(2,1)S(1)} %pool.1), channel_id=1, replica_groups=mesh['rep'=16,'loop'=8,'seq'=2] {'loop','seq'}, dimensions={0} | all-to-all | bytes 294912 | tf_op jit(solution)/shard_map/all_to_all | solution.py:269
  19.2 0.0 copy-done
  19.2 1.5 %pairs.1 = (f32[4,576]{1,0:T(4,128)S(1)}, bf16[16,8,768]{2,1,0:T(8,128)(2,1)S(1)}) custom-call(bf16[16,4,1152]{2,1,0:T(4,128)(2,1)S(1)} %all_to_all.10.gathered, bf16[1152,1152]{1,0:T(8,128)(2,1)S(1)} %copy-done), custom_call_target="tpu_custom_call" | custom-call | tf_op jit(solution)/shard_map/pairs/pallas_call | solution.py:271
  20.7 21.4 %all_to_all.11.blocks = bf16[16,8,768]{2,1,0:T(8,128)(2,1)S(1)} all-to-all(bf16[16,8,768]{2,1,0:T(8,128)(2,1)S(1)} %get-tuple-element.10), channel_id=1, replica_groups=mesh['rep'=16,'loop'=8,'seq'=2] {'rep'}, dimensions={0} | all-to-all | bytes 393216 | tf_op jit(solution)/shard_map/all_to_all | solution.py:287
  42.1 0.7 %sums.1 = (f32[9,576]{1,0:T(8,128)}, f32[4,576]{1,0:T(4,128)}) custom-call(bf16[16,8,768]{2,1,0:T(8,128)(2,1)S(1)} %all_to_all.11.blocks, f32[4,576]{1,0:T(4,128)S(1)} %get-tuple-element.11.text_sums), custom_call_target="tpu_custom_call" | custom-call | tf_op jit(solution)/shard_map/sums/pallas_call | solution.py:288
Async XLA Ops:
  0.6 18.5 %copy-start = (bf16[1152,1152]{1,0:T(8,128)(2,1)S(1)}, bf16[1152,1152]{1,0:T(8,128)(2,1)}, u32[]{:S(2)}) copy-start(bf16[1152,1152]{1,0:T(8,128)(2,1)} %w_out) | copy-start | bytes 7962628

commit v5 on v4

--- a/solution.py
+++ b/solution.py
@@ -25,6 +25,7 @@
 OWN_ROWS = 9
 FOLD = 8
 FOLD_AT = 640
+Z_ORDER = (4, 5, 6, 7, 3, 2, 1, 0)
 MESSAGE = 768
 
 BF16 = jnp.bfloat16
@@ -164,9 +165,11 @@
 
 def pair_kernel(gathered, w_out, txt_grad, partial, pair_rows, pooled_rows, folded):
     members = gathered.shape[0]
+    groups = lax.axis_size("yh")
+    group = lax.axis_index("yh")
     images = IMAGES * members
-    loops = members // 2
-    own_rows = images // loops
+    loops = members // (2 * groups)
+    own_rows = images // (loops * groups)
     half = WIDTH // 2
     loop_index = lax.axis_index("loop")
     first = lax.axis_index("seq") == 0
@@ -175,9 +178,9 @@
     block = gathered[...].astype(F32).reshape(members * height, WIDTH).astype(BF16)
     row = lax.broadcasted_iota(jnp.int32, (images, members * height), 0)
     source = lax.broadcasted_iota(jnp.int32, (images, members * height), 1)
-    pick_image = source == (row // IMAGES) * height + row % IMAGES
-    text_source = (row // own_rows) * 2 * height + IMAGES + (row % own_rows) // 2
-    pick = [pick_image, source == text_source, source == text_source + height]
+    pick_image = source == (members - 1 - row // IMAGES) * height + row % IMAGES
+    text_source = (members - 1 - (row // own_rows) * 2) * height + IMAGES + (row % own_rows) // 2
+    pick = [pick_image, source == text_source, source == text_source - height]
     pick = jnp.concatenate([one.astype(F32) for one in pick], axis=0).astype(BF16)
     compact = dot(pick, block)
     pooled_f32 = compact[:images]
@@ -200,7 +203,12 @@
         jnp.int32, (images, images), 1
     )
     labels = jnp.where(same, 1.0, -1.0)
-    pair_grad = (LOGIT_SCALE * (-labels * jax.nn.sigmoid(-labels * logit))).astype(BF16)
+    block_size = images // groups
+    together = lax.broadcasted_iota(jnp.int32, (images, images), 0) // block_size == (
+        lax.broadcasted_iota(jnp.int32, (images, images), 1) // block_size
+    )
+    pair_grad = LOGIT_SCALE * (-labels * jax.nn.sigmoid(-labels * logit))
+    pair_grad = jnp.where(together, pair_grad, 0.0).astype(BF16)
     image_grad = dot(pair_grad, texts)
     inner = jnp.sum(unit * image_grad, axis=1, keepdims=True)
     out_grad = ((image_grad - unit * inner) / length).astype(F32)
@@ -208,10 +216,10 @@
 
     reps = partial.shape[0]
     stride = loops * OWN_ROWS
-    start = OWN_ROWS * loop_index
+    start = stride * reps * group + OWN_ROWS * loop_index
     rows = jnp.concatenate(
-        [pooled_rows[pl.ds(stride * rep + start, FOLD), :] for rep in range(reps)]
-        + [pooled_rows[pl.ds(stride * rep + start + FOLD, 1), :] for rep in range(reps)],
+        [pooled_rows[pl.ds(stride * rep + start, FOLD), :] for rep in Z_ORDER]
+        + [pooled_rows[pl.ds(stride * rep + start + FOLD, 1), :] for rep in Z_ORDER],
         axis=0,
     ).astype(BF16)
     padded = jnp.concatenate([out_half, jnp.zeros((images, FOLD_AT - half), BF16)], axis=1)
@@ -225,7 +233,7 @@
 
     pair_rows[:images] = jnp.transpose(pair_grad.astype(F32))
     pair_rows[images:] = jnp.zeros((pair_rows.shape[0] - images, images), F32)
-    own = dot(pair_rows[pl.ds(own_rows * loop_index, 8), :].astype(BF16), embedded)
+    own = dot(pair_rows[pl.ds(block_size * group + own_rows * loop_index, 8), :].astype(BF16), embedded)
     txt_grad[...] = jnp.where(first, own[:own_rows, :half], own[:own_rows, half:])
 
 
@@ -266,7 +274,7 @@
         compiler_params=pltpu.CompilerParams(vmem_limit_bytes=60 * 1024 * 1024),
     )(counts, positions, probe, jnp.asarray(angle_table()), texts, patches, w_keyval)
     message, w_out = lax.optimization_barrier((message, w_out))
-    gathered = lax.all_to_all(message, ("loop", "seq"), split_axis=0, concat_axis=0, tiled=True)
+    gathered = lax.all_to_all(message, ("yh", "loop", "seq"), split_axis=0, concat_axis=0, tiled=True, axis_index_groups=[list(range(members))[::-1]])
     images = IMAGES * members
     txt_grad, partial = pl.pallas_call(
         pair_kernel,
@@ -284,7 +292,7 @@
         ],
         compiler_params=pltpu.CompilerParams(vmem_limit_bytes=24 * 1024 * 1024),
     )(gathered, w_out)
-    blocks = lax.all_to_all(partial, "rep", split_axis=0, concat_axis=0, tiled=True)
+    blocks = lax.all_to_all(partial, "z", split_axis=0, concat_axis=0, tiled=True, axis_index_groups=[list(Z_ORDER)])
     wo_grad, txt_grad = pl.pallas_call(
         sum_kernel,
         name="sums",
@@ -300,20 +308,23 @@
 
 
 def solution(mesh):
-    reps = mesh.shape["rep"]
-    members = mesh.shape["loop"] * mesh.shape["seq"]
+    split = (2, mesh.shape["rep"] // 2, mesh.shape["loop"], mesh.shape["seq"])
+    mesh = jax.sharding.Mesh(mesh.devices.reshape(split), ("yh", "z", "loop", "seq"))
+    reps = mesh.shape["z"]
+    members = mesh.shape["yh"] * mesh.shape["loop"] * mesh.shape["seq"]
+    every = ("yh", "z", "loop", "seq")
     return jax.shard_map(
         functools.partial(local, reps, members),
         mesh=mesh,
         in_specs=(
-            P(("rep", "loop", "seq"), None, None),
-            P(None, ("rep", "loop", "seq"), None),
-            P(("rep", "loop", "seq")),
+            P(every, None, None),
+            P(None, every, None),
+            P(every),
             P(),
             P(),
             P(),
-            P(("rep", "loop"), "seq"),
+            P(("yh", "z", "loop"), "seq"),
         ),
-        out_specs=(P(("rep", "loop"), "seq"), P(("rep", "loop"), "seq")),
+        out_specs=(P(("yh", "z", "loop"), "seq"), P(("yh", "z", "loop"), "seq")),
         check_vma=False,
     )

time: 42.9 us -> 36.8 us (0.86); the launches traced: 42.8 us -> 36.2 us
  blocking collectives: 33.6 us -> 26.9 us
    all_to_all x2, blocking collectives: 33.6 us -> 26.9 us  [the longest x1 14.1 us: local(): lax.all_to_all(message, ('yh', 'loop', 'seq'), split_axis=0, concat_axis=...]
where the time goes in v5:
time: 36.8 us; the launch traced here: 36.2 us
  blocking collectives  26.9 us (73%)
  Pallas kernels  8.59 us (23%)
  between operations  0.66 us (2%)
    all_to_all x1, blocking collectives, local(): lax.all_to_all(message, ('yh', 'loop', 'seq'), split_axis=0, concat_axis=...  14.1 us
    all_to_all x1, blocking collectives, local(): lax.all_to_all(partial, 'z', split_axis=0, concat_axis=0, tiled=True, axi...  12.8 us
    pallas_call x1, Pallas kernels, local(): pl.pallas_call(pool_kernel, name='pool', out_shape=pltpu.VMEM((members, I...  6.28 us
    pallas_call x1, Pallas kernels, local(): pl.pallas_call(pair_kernel, name='pairs', out_shape=(pltpu.VMEM(texts.sha...  1.6 us

profile of v5, /device:TPU:32, one launch (start us, length us, event | category | flops | bytes accessed | tf_op | source)
XLA Modules:
  0.0 36.2 jit_solution(4265673561245352710)
XLA Ops:
  0.6 0.0 copy-start
  0.6 6.3 %pool.1 = bf16[32,4,1152]{2,1,0:T(4,128)(2,1)S(1)} custom-call(s32[2]{0:T(128)} %counts_hbm.1, s32[2,2,256]{2,1,0:T(2,128)} %positions_hbm.1, bf16[1152]{0:T(1024)(128)(2,1)} %probe_hbm.1, f32[256,256]{1,0:T(8,128)} %constant.2.clone.table_hbm, bf16[4,576]{1,0:T(4,128)(2,1)} %texts_hbm.1, bf16[2,256,1152]{2,1,0:T(8,128)(2,1)} %patches_hbm.1, ...), custom_call_target="tpu_custom_call" | custom-call | tf_op jit(solution)/shard_map/pool/pallas_call | solution.py:254
  6.9 14.1 %all_to_all.10.gathered = bf16[32,4,1152]{2,1,0:T(4,128)(2,1)S(1)} all-to-all(bf16[32,4,1152]{2,1,0:T(4,128)(2,1)S(1)} %pool.1), channel_id=1, replica_groups={{143,142,141,140,139,138,137,136,135,134,133,132,131,130,129,128,15,14,..., dimensions={0} | all-to-all | bytes 589824 | tf_op jit(solution)/shard_map/all_to_all | solution.py:277
  21.0 0.0 copy-done
  21.0 1.6 %pairs.1 = (f32[4,576]{1,0:T(4,128)S(1)}, bf16[8,8,768]{2,1,0:T(8,128)(2,1)S(1)}) custom-call(bf16[32,4,1152]{2,1,0:T(4,128)(2,1)S(1)} %all_to_all.10.gathered, bf16[1152,1152]{1,0:T(8,128)(2,1)S(1)} %copy-done), custom_call_target="tpu_custom_call" | custom-call | tf_op jit(solution)/shard_map/pairs/pallas_call | solution.py:279
  22.6 12.8 %all_to_all.11.blocks = bf16[8,8,768]{2,1,0:T(8,128)(2,1)S(1)} all-to-all(bf16[8,8,768]{2,1,0:T(8,128)(2,1)S(1)} %get-tuple-element.10), channel_id=1, replica_groups={{64,80,96,112,48,32,16,0},{65,81,97,113,49,33,17,1},{66,82,98,114,50,34..., dimensions={0} | all-to-all | bytes 196608 | tf_op jit(solution)/shard_map/all_to_all | solution.py:295
  35.5 0.7 %sums.1 = (f32[9,576]{1,0:T(8,128)}, f32[4,576]{1,0:T(4,128)}) custom-call(bf16[8,8,768]{2,1,0:T(8,128)(2,1)S(1)} %all_to_all.11.blocks, f32[4,576]{1,0:T(4,128)S(1)} %get-tuple-element.11.text_sums), custom_call_target="tpu_custom_call" | custom-call | tf_op jit(solution)/shard_map/sums/pallas_call | solution.py:296
Async XLA Ops:
  0.6 20.4 %copy-start = (bf16[1152,1152]{1,0:T(8,128)(2,1)S(1)}, bf16[1152,1152]{1,0:T(8,128)(2,1)}, u32[]{:S(2)}) copy-start(bf16[1152,1152]{1,0:T(8,128)(2,1)} %w_out) | copy-start | bytes 7962628

commit v6 on v5

--- a/solution.py
+++ b/solution.py
@@ -25,7 +25,15 @@
 OWN_ROWS = 9
 FOLD = 8
 FOLD_AT = 640
-Z_ORDER = (4, 5, 6, 7, 3, 2, 1, 0)
+MEMBER_ORDER = tuple(
+    16 * y_hi + 4 * x + 2 * core + y_lo
+    for x in (3, 2, 1, 0)
+    for y_hi in (1, 0)
+    for y_lo in (1, 0)
+    for core in (1, 0)
+)
+REP_ORDER = (4, 5, 6, 7, 3, 2, 1, 0)
+KEY_PARTS = ((0, 512), (512, 1152))
 MESSAGE = 768
 
 BF16 = jnp.bfloat16
@@ -45,6 +53,19 @@
     return table
 
 
+def pick_table(members):
+    height = 2 * IMAGES
+    images = IMAGES * members
+    at = {member: place * height for place, member in enumerate(MEMBER_ORDER)}
+    table = np.zeros((3 * images, members * height), np.float32)
+    for n in range(images):
+        table[n, at[n // IMAGES] + n % IMAGES] = 1
+        for half in range(2):
+            place = at[n // 4 * 2 + half] + IMAGES + n % 4 // 2
+            table[(1 + half) * images + n, place] = 1
+    return table
+
+
 def dot(left, right, left_axis=1, right_axis=0):
     return lax.dot_general(
         left, right, (((left_axis,), (right_axis,)), ((), ())), preferred_element_type=F32
@@ -57,9 +78,10 @@
 
 
 def pool_kernel(
-    counts_hbm, positions_hbm, probe_hbm, table_hbm, texts_hbm, patches_hbm, weights_hbm, out,
-    counts, positions, probe, table, texts, patches, w_key, w_val,
-    small_sem, patch_sem, key_sem, val_sem,
+    counts_hbm, positions_hbm, probe_hbm, table_hbm, texts_hbm, patches_hbm, weights_hbm, w_out_hbm,
+    out, w_out,
+    counts, positions, probe, table, texts, turn, patches, w_key, w_val,
+    small_sem, patch_sem, key_sem, val_sem, out_sem,
 ):
     small = [
         pltpu.make_async_copy(source, target, small_sem.at[n])
@@ -81,11 +103,15 @@
         )
         for image in range(IMAGES)
     ]
-    copies.append(
-        pltpu.make_async_copy(weights_hbm.at[:, pl.ds(0, WIDTH)], w_key, key_sem)
-    )
+    key_copies = [
+        pltpu.make_async_copy(
+            weights_hbm.at[:, pl.ds(lo, hi - lo)], w_key.at[:, pl.ds(lo, hi - lo)], key_sem.at[n]
+        )
+        for n, (lo, hi) in enumerate(KEY_PARTS)
+    ]
     val_copy = pltpu.make_async_copy(weights_hbm.at[:, pl.ds(WIDTH, WIDTH)], w_val, val_sem)
-    for copy in small + copies + [val_copy]:
+    out_copy = pltpu.make_async_copy(w_out_hbm, w_out, out_sem)
+    for copy in small + copies + key_copies + [val_copy, out_copy]:
         copy.start()
     for copy in small:
         copy.wait()
@@ -126,11 +152,18 @@
     head_cols = (head_row >= head_lane) & (head_row < head_lane + HEAD_DIM)
     head_cols = head_cols.astype(F32).astype(BF16)
 
-    for copy in copies:
+    turn[...] = dot(cos_sin, spread)
+    for copy in copies + key_copies[:1]:
         copy.wait()
-    keys = dot(patches[...], w_key[...])
-    high, low = split(keys * dot(cos_sin, spread))
-    scores = jnp.transpose(dot(high, head_cols) + dot(low, head_cols)) * HEAD_DIM ** (-0.5)
+    first_keys = dot(patches[...], w_key[:, : KEY_PARTS[0][1]])
+    key_copies[1].wait()
+    scores = jnp.zeros((IMAGES * SLOTS, HEADS), F32)
+    for lo, hi in KEY_PARTS:
+        keys = first_keys if lo == 0 else dot(patches[...], w_key[:, lo:hi])
+        high, low = split(keys * turn[:, lo:hi])
+        cols = head_cols[lo:hi]
+        scores += dot(high, cols) + dot(low, cols)
+    scores = jnp.transpose(scores) * HEAD_DIM ** (-0.5)
 
     slot = lax.broadcasted_iota(jnp.int32, (HEADS, SLOTS), 1)
     sums, totals = [], []
@@ -161,9 +194,10 @@
     message = jnp.concatenate(pooled + pairs, axis=0).astype(BF16)
     for peer in range(out.shape[0]):
         out[peer] = message
-
-
-def pair_kernel(gathered, w_out, txt_grad, partial, pair_rows, pooled_rows, folded):
+    out_copy.wait()
+
+
+def pair_kernel(gathered, w_out, pick_ref, txt_grad, partial, pair_rows, pooled_rows, folded):
     members = gathered.shape[0]
     groups = lax.axis_size("yh")
     group = lax.axis_index("yh")
@@ -176,12 +210,7 @@
 
     height = gathered.shape[1]
     block = gathered[...].astype(F32).reshape(members * height, WIDTH).astype(BF16)
-    row = lax.broadcasted_iota(jnp.int32, (images, members * height), 0)
-    source = lax.broadcasted_iota(jnp.int32, (images, members * height), 1)
-    pick_image = source == (members - 1 - row // IMAGES) * height + row % IMAGES
-    text_source = (members - 1 - (row // own_rows) * 2) * height + IMAGES + (row % own_rows) // 2
-    pick = [pick_image, source == text_source, source == text_source - height]
-    pick = jnp.concatenate([one.astype(F32) for one in pick], axis=0).astype(BF16)
+    pick = pick_ref[...].astype(BF16)
     compact = dot(pick, block)
     pooled_f32 = compact[:images]
     pooled = pooled_f32.astype(BF16)
@@ -218,8 +247,8 @@
     stride = loops * OWN_ROWS
     start = stride * reps * group + OWN_ROWS * loop_index
     rows = jnp.concatenate(
-        [pooled_rows[pl.ds(stride * rep + start, FOLD), :] for rep in Z_ORDER]
-        + [pooled_rows[pl.ds(stride * rep + start + FOLD, 1), :] for rep in Z_ORDER],
+        [pooled_rows[pl.ds(stride * rep + start, FOLD), :] for rep in REP_ORDER]
+        + [pooled_rows[pl.ds(stride * rep + start + FOLD, 1), :] for rep in REP_ORDER],
         axis=0,
     ).astype(BF16)
     padded = jnp.concatenate([out_half, jnp.zeros((images, FOLD_AT - half), BF16)], axis=1)
@@ -248,33 +277,43 @@
     )
 
 
+def exchange(value, axis, order):
+    return lax.all_to_all(
+        value, axis, split_axis=0, concat_axis=0, tiled=True, axis_index_groups=[list(order)]
+    )
+
+
 def local(reps, members, patches, positions, counts, probe, w_keyval, w_out, texts):
     vmem = pl.BlockSpec(memory_space=pltpu.VMEM)
     hbm = pl.BlockSpec(memory_space=pltpu.HBM)
-    message = pl.pallas_call(
+    message, w_out = pl.pallas_call(
         pool_kernel,
         name="pool",
-        out_shape=pltpu.VMEM((members, IMAGES + texts.shape[0] // 2, WIDTH), BF16),
-        in_specs=[hbm] * 7,
-        out_specs=vmem,
+        out_shape=(
+            pltpu.VMEM((members, IMAGES + texts.shape[0] // 2, WIDTH), BF16),
+            pltpu.VMEM(w_out.shape, BF16),
+        ),
+        in_specs=[hbm] * 8,
+        out_specs=(vmem, vmem),
         scratch_shapes=[
             pltpu.SMEM((IMAGES,), jnp.int32),
             pltpu.VMEM(positions.shape, jnp.int32),
             pltpu.VMEM(probe.shape, BF16),
             pltpu.VMEM((2 * POSITIONS, 2 * POSITIONS), F32),
             pltpu.VMEM(texts.shape, BF16),
+            pltpu.VMEM((IMAGES * SLOTS, WIDTH), F32),
             pltpu.VMEM((IMAGES * SLOTS, WIDTH), BF16),
             pltpu.VMEM((WIDTH, WIDTH), BF16),
             pltpu.VMEM((WIDTH, WIDTH), BF16),
             pltpu.SemaphoreType.DMA((5,)),
             pltpu.SemaphoreType.DMA((IMAGES,)),
+            pltpu.SemaphoreType.DMA((len(KEY_PARTS),)),
             pltpu.SemaphoreType.DMA,
             pltpu.SemaphoreType.DMA,
         ],
         compiler_params=pltpu.CompilerParams(vmem_limit_bytes=60 * 1024 * 1024),
-    )(counts, positions, probe, jnp.asarray(angle_table()), texts, patches, w_keyval)
-    message, w_out = lax.optimization_barrier((message, w_out))
-    gathered = lax.all_to_all(message, ("yh", "loop", "seq"), split_axis=0, concat_axis=0, tiled=True, axis_index_groups=[list(range(members))[::-1]])
+    )(counts, positions, probe, jnp.asarray(angle_table()), texts, patches, w_keyval, w_out)
+    gathered = exchange(message, ("yh", "loop", "seq"), MEMBER_ORDER)
     images = IMAGES * members
     txt_grad, partial = pl.pallas_call(
         pair_kernel,
@@ -283,7 +322,7 @@
             pltpu.VMEM(texts.shape, F32),
             pltpu.VMEM((reps, FOLD, MESSAGE), BF16),
         ),
-        in_specs=[vmem, vmem],
+        in_specs=[vmem, vmem, vmem],
         out_specs=(vmem, vmem),
         scratch_shapes=[
             pltpu.VMEM((images + 8, images), F32),
@@ -291,8 +330,8 @@
             pltpu.VMEM((reps * FOLD, MESSAGE - FOLD_AT), F32),
         ],
         compiler_params=pltpu.CompilerParams(vmem_limit_bytes=24 * 1024 * 1024),
-    )(gathered, w_out)
-    blocks = lax.all_to_all(partial, "z", split_axis=0, concat_axis=0, tiled=True, axis_index_groups=[list(Z_ORDER)])
+    )(gathered, w_out, jnp.asarray(pick_table(members)))
+    blocks = exchange(partial, "z", REP_ORDER)
     wo_grad, txt_grad = pl.pallas_call(
         sum_kernel,
         name="sums",

time: 36.8 us -> 36.2 us (0.984)
  Pallas kernels: 8.59 us -> 8.05 us
    pallas_call x1, Pallas kernels: 6.28 us -> 5.78 us  [local(): pl.pallas_call(pool_kernel, name='pool', out_shape=(pltpu.VMEM((members,...]
where the time goes in v6:
time: 36.2 us; the launch traced here: 35.6 us
  blocking collectives  26.9 us (74%)
  Pallas kernels  8.05 us (22%)
  between operations  0.66 us (2%)
    all_to_all x2, blocking collectives, exchange(): lax.all_to_all(value, axis, split_axis=0, concat_axis=0, tiled=True, axis...  26.9 us
    pallas_call x1, Pallas kernels, local(): pl.pallas_call(pool_kernel, name='pool', out_shape=(pltpu.VMEM((members,...  5.78 us
    pallas_call x1, Pallas kernels, local(): pl.pallas_call(pair_kernel, name='pairs', out_shape=(pltpu.VMEM(texts.sha...  1.57 us

profile of v6, /device:TPU:32, one launch (start us, length us, event | category | flops | bytes accessed | tf_op | source)
XLA Modules:
  0.0 35.6 jit_solution(3895681974446930914)
XLA Ops:
  0.6 0.0 copy-start
  0.6 5.8 %pool.1 = (bf16[32,4,1152]{2,1,0:T(4,128)(2,1)S(1)}, bf16[1152,1152]{1,0:T(8,128)(2,1)S(1)}) custom-call(s32[2]{0:T(128)} %counts_hbm.1, s32[2,2,256]{2,1,0:T(2,128)} %positions_hbm.1, bf16[1152]{0:T(1024)(128)(2,1)} %probe_hbm.1, f32[256,256]{1,0:T(8,128)} %constant.4.clone.table_hbm, bf16[4,576]{1,0:T(4,128)(2,1)} %texts_hbm.1, ...), custom_call_target="tpu_custom_call" | custom-call | tf_op jit(solution)/shard_map/pool/pallas_call | solution.py:289
  6.4 14.1 %all_to_all.10.gathered = bf16[32,4,1152]{2,1,0:T(4,128)(2,1)S(1)} all-to-all(bf16[32,4,1152]{2,1,0:T(4,128)(2,1)S(1)} %get-tuple-element.8), channel_id=1, replica_groups={{143,141,142,140,15,13,14,12,139,137,138,136,11,9,10,8,135,133,134,132,..., dimensions={0} | all-to-all | bytes 589824 | tf_op jit(solution)/shard_map/all_to_all | solution.py:281
  20.5 0.0 copy-done
  20.5 1.6 %pairs.1 = (f32[4,576]{1,0:T(4,128)S(1)}, bf16[8,8,768]{2,1,0:T(8,128)(2,1)S(1)}) custom-call(bf16[32,4,1152]{2,1,0:T(4,128)(2,1)S(1)} %all_to_all.10.gathered, bf16[1152,1152]{1,0:T(8,128)(2,1)S(1)} %get-tuple-element.9.w_out, f32[192,128]{1,0:T(8,128)S(1)} %copy-done), custom_call_target="tpu_custom_call" | custom-call | tf_op jit(solution)/shard_map/pairs/pallas_call | solution.py:318
  22.1 12.8 %all_to_all.11.blocks = bf16[8,8,768]{2,1,0:T(8,128)(2,1)S(1)} all-to-all(bf16[8,8,768]{2,1,0:T(8,128)(2,1)S(1)} %get-tuple-element.10), channel_id=1, replica_groups={{64,80,96,112,48,32,16,0},{65,81,97,113,49,33,17,1},{66,82,98,114,50,34..., dimensions={0} | all-to-all | bytes 196608 | tf_op jit(solution)/shard_map/all_to_all | solution.py:281
  34.9 0.7 %sums.1 = (f32[9,576]{1,0:T(8,128)}, f32[4,576]{1,0:T(4,128)}) custom-call(bf16[8,8,768]{2,1,0:T(8,128)(2,1)S(1)} %all_to_all.11.blocks, f32[4,576]{1,0:T(4,128)S(1)} %get-tuple-element.11.text_sums), custom_call_target="tpu_custom_call" | custom-call | tf_op jit(solution)/shard_map/sums/pallas_call | solution.py:335
Async XLA Ops:
  0.6 19.9 %copy-start = (f32[192,128]{1,0:T(8,128)S(1)}, f32[192,128]{1,0:T(8,128)}, u32[]{:S(2)}) copy-start(f32[192,128]{1,0:T(8,128)} %constant.5.clone.pick_ref) | copy-start | bytes 294916

commit v7 on v6

--- a/solution.py
+++ b/solution.py
@@ -27,7 +27,7 @@
 FOLD_AT = 640
 MEMBER_ORDER = tuple(
     16 * y_hi + 4 * x + 2 * core + y_lo
-    for x in (3, 2, 1, 0)
+    for x in (2, 3, 1, 0)
     for y_hi in (1, 0)
     for y_lo in (1, 0)
     for core in (1, 0)

time: 36.2 us -> 35.7 us (0.986)
  the two profiles are of different devices: /device:TPU:32 before, /device:TPU:1 now
where the time goes in v7:
time: 35.7 us; the launch traced here: 35.6 us
  blocking collectives  26.9 us (75%)
  Pallas kernels  8.05 us (23%)
  between operations  0.66 us (2%)
    all_to_all x2, blocking collectives, exchange(): lax.all_to_all(value, axis, split_axis=0, concat_axis=0, tiled=True, axis...  26.9 us
    pallas_call x1, Pallas kernels, local(): pl.pallas_call(pool_kernel, name='pool', out_shape=(pltpu.VMEM((members,...  5.78 us
    pallas_call x1, Pallas kernels, local(): pl.pallas_call(pair_kernel, name='pairs', out_shape=(pltpu.VMEM(texts.sha...  1.57 us

profile of v7, /device:TPU:1, one launch (start us, length us, event | category | flops | bytes accessed | tf_op | source)
XLA Modules:
  0.0 35.6 jit_solution(13227593316977488754)
XLA Ops:
  0.6 0.0 copy-start
  0.6 5.8 %pool.1 = (bf16[32,4,1152]{2,1,0:T(4,128)(2,1)S(1)}, bf16[1152,1152]{1,0:T(8,128)(2,1)S(1)}) custom-call(s32[2]{0:T(128)} %counts_hbm.1, s32[2,2,256]{2,1,0:T(2,128)} %positions_hbm.1, bf16[1152]{0:T(1024)(128)(2,1)} %probe_hbm.1, f32[256,256]{1,0:T(8,128)} %constant.4.clone.table_hbm, bf16[4,576]{1,0:T(4,128)(2,1)} %texts_hbm.1, ...), custom_call_target="tpu_custom_call" | custom-call | tf_op jit(solution)/shard_map/pool/pallas_call | solution.py:289
  6.4 14.6 %all_to_all.10.gathered = bf16[32,4,1152]{2,1,0:T(4,128)(2,1)S(1)} all-to-all(bf16[32,4,1152]{2,1,0:T(4,128)(2,1)S(1)} %get-tuple-element.8), channel_id=1, replica_groups={{139,137,138,136,11,9,10,8,143,141,142,140,15,13,14,12,135,133,134,132,..., dimensions={0} | all-to-all | bytes 589824 | tf_op jit(solution)/shard_map/all_to_all | solution.py:281
  21.1 0.0 copy-done
  21.1 1.6 %pairs.1 = (f32[4,576]{1,0:T(4,128)S(1)}, bf16[8,8,768]{2,1,0:T(8,128)(2,1)S(1)}) custom-call(bf16[32,4,1152]{2,1,0:T(4,128)(2,1)S(1)} %all_to_all.10.gathered, bf16[1152,1152]{1,0:T(8,128)(2,1)S(1)} %get-tuple-element.9.w_out, f32[192,128]{1,0:T(8,128)S(1)} %copy-done), custom_call_target="tpu_custom_call" | custom-call | tf_op jit(solution)/shard_map/pairs/pallas_call | solution.py:318
  22.6 12.2 %all_to_all.11.blocks = bf16[8,8,768]{2,1,0:T(8,128)(2,1)S(1)} all-to-all(bf16[8,8,768]{2,1,0:T(8,128)(2,1)S(1)} %get-tuple-element.10), channel_id=1, replica_groups={{64,80,96,112,48,32,16,0},{65,81,97,113,49,33,17,1},{66,82,98,114,50,34..., dimensions={0} | all-to-all | bytes 196608 | tf_op jit(solution)/shard_map/all_to_all | solution.py:281
  34.9 0.7 %sums.1 = (f32[9,576]{1,0:T(8,128)}, f32[4,576]{1,0:T(4,128)}) custom-call(bf16[8,8,768]{2,1,0:T(8,128)(2,1)S(1)} %all_to_all.11.blocks, f32[4,576]{1,0:T(4,128)S(1)} %get-tuple-element.11.text_sums), custom_call_target="tpu_custom_call" | custom-call | tf_op jit(solution)/shard_map/sums/pallas_call | solution.py:335
Async XLA Ops:
  0.6 20.4 %copy-start = (f32[192,128]{1,0:T(8,128)S(1)}, f32[192,128]{1,0:T(8,128)}, u32[]{:S(2)}) copy-start(f32[192,128]{1,0:T(8,128)} %constant.5.clone.pick_ref) | copy-start | bytes 294916

commit v8 on v7

--- a/solution.py
+++ b/solution.py
@@ -27,7 +27,7 @@
 FOLD_AT = 640
 MEMBER_ORDER = tuple(
     16 * y_hi + 4 * x + 2 * core + y_lo
-    for x in (2, 3, 1, 0)
+    for x in (2, 1, 3, 0)
     for y_hi in (1, 0)
     for y_lo in (1, 0)
     for core in (1, 0)

time: 35.7 us -> 35.7 us (level)
  the two profiles are of different devices: /device:TPU:1 before, /device:TPU:32 now
where the time goes in v8:
time: 35.7 us; the launch traced here: 35 us
  blocking collectives  26.3 us (74%)
  Pallas kernels  8.05 us (23%)
  between operations  0.66 us (2%)
    all_to_all x2, blocking collectives, exchange(): lax.all_to_all(value, axis, split_axis=0, concat_axis=0, tiled=True, axis...  26.3 us
    pallas_call x1, Pallas kernels, local(): pl.pallas_call(pool_kernel, name='pool', out_shape=(pltpu.VMEM((members,...  5.78 us
    pallas_call x1, Pallas kernels, local(): pl.pallas_call(pair_kernel, name='pairs', out_shape=(pltpu.VMEM(texts.sha...  1.56 us

profile of v8, /device:TPU:32, one launch (start us, length us, event | category | flops | bytes accessed | tf_op | source)
XLA Modules:
  0.0 35.0 jit_solution(17100393529300659210)
XLA Ops:
  0.6 0.0 copy-start
  0.6 5.8 %pool.1 = (bf16[32,4,1152]{2,1,0:T(4,128)(2,1)S(1)}, bf16[1152,1152]{1,0:T(8,128)(2,1)S(1)}) custom-call(s32[2]{0:T(128)} %counts_hbm.1, s32[2,2,256]{2,1,0:T(2,128)} %positions_hbm.1, bf16[1152]{0:T(1024)(128)(2,1)} %probe_hbm.1, f32[256,256]{1,0:T(8,128)} %constant.4.clone.table_hbm, bf16[4,576]{1,0:T(4,128)(2,1)} %texts_hbm.1, ...), custom_call_target="tpu_custom_call" | custom-call | tf_op jit(solution)/shard_map/pool/pallas_call | solution.py:289
  6.4 13.5 %all_to_all.10.gathered = bf16[32,4,1152]{2,1,0:T(4,128)(2,1)S(1)} all-to-all(bf16[32,4,1152]{2,1,0:T(4,128)(2,1)S(1)} %get-tuple-element.8), channel_id=1, replica_groups={{139,137,138,136,11,9,10,8,135,133,134,132,7,5,6,4,143,141,142,140,15,1..., dimensions={0} | all-to-all | bytes 589824 | tf_op jit(solution)/shard_map/all_to_all | solution.py:281
  19.9 0.0 copy-done
  19.9 1.6 %pairs.1 = (f32[4,576]{1,0:T(4,128)S(1)}, bf16[8,8,768]{2,1,0:T(8,128)(2,1)S(1)}) custom-call(bf16[32,4,1152]{2,1,0:T(4,128)(2,1)S(1)} %all_to_all.10.gathered, bf16[1152,1152]{1,0:T(8,128)(2,1)S(1)} %get-tuple-element.9.w_out, f32[192,128]{1,0:T(8,128)S(1)} %copy-done), custom_call_target="tpu_custom_call" | custom-call | tf_op jit(solution)/shard_map/pairs/pallas_call | solution.py:318
  21.5 12.8 %all_to_all.11.blocks = bf16[8,8,768]{2,1,0:T(8,128)(2,1)S(1)} all-to-all(bf16[8,8,768]{2,1,0:T(8,128)(2,1)S(1)} %get-tuple-element.10), channel_id=1, replica_groups={{64,80,96,112,48,32,16,0},{65,81,97,113,49,33,17,1},{66,82,98,114,50,34..., dimensions={0} | all-to-all | bytes 196608 | tf_op jit(solution)/shard_map/all_to_all | solution.py:281
  34.3 0.7 %sums.1 = (f32[9,576]{1,0:T(8,128)}, f32[4,576]{1,0:T(4,128)}) custom-call(bf16[8,8,768]{2,1,0:T(8,128)(2,1)S(1)} %all_to_all.11.blocks, f32[4,576]{1,0:T(4,128)S(1)} %get-tuple-element.11.text_sums), custom_call_target="tpu_custom_call" | custom-call | tf_op jit(solution)/shard_map/sums/pallas_call | solution.py:335
Async XLA Ops:
  0.6 19.3 %copy-start = (f32[192,128]{1,0:T(8,128)S(1)}, f32[192,128]{1,0:T(8,128)}, u32[]{:S(2)}) copy-start(f32[192,128]{1,0:T(8,128)} %constant.5.clone.pick_ref) | copy-start | bytes 294916
